TPU v7x, 512 devices: a whole 4x8x8 slice. The times are simulated.
512 devices in a mesh: aux: 32 (over z_lo, y), basis: 16 (over z_hi, x, core).
Axes of the slice: x: 4, y: 8, z: 8 (z_hi: 2, z_lo: 4; z = z_hi * 4 + z_lo), core: 2. Of those that a mesh axis runs over, the one named last changes fastest.
Arguments:
- factors: bfloat16 [128, 500, 8192], P('aux', None, 'basis'), may hold values from -0.1875 to 0.1875
Outputs:
- exchange_band: float32 [3, 8192, 512], P(None, ('basis', 'aux'))
All inputs are finite; a program needn't handle non-finite values.
Results may differ from a plain program's by a relative error of at most 0.0003.
Values may be sent and summed in bfloat16 or wider, within the bound.
No kernel may reach another device: no remote copies, remote signals or barrier semaphores. Data moves between devices by JAX's collectives and lax.ppermute only.
A program may use at most 64 MiB of HBM per device.

v0:
```python
import jax
import jax.numpy as jnp
from jax import lax
from jax.sharding import PartitionSpec as P

SHIFTS = 3


def from_behind(value, axis, steps):
    count = lax.axis_size(axis)
    pairs = [(source, (source + steps) % count) for source in range(count)]
    return lax.ppermute(value, axis, pairs)


def form_tile(own_flat, moving):
    other = moving.reshape(-1, moving.shape[2])
    return lax.dot_general(
        own_flat, other, (((0,), (0,)), ((), ())), preferred_element_type=jnp.float32
    )


def on_device(factors):
    own_flat = factors.reshape(-1, factors.shape[2])
    moving = factors
    results = []
    for s in range(SHIFTS):
        if s > 0:
            moving = from_behind(moving, "basis", -1)
        partial_tile = form_tile(own_flat, moving)
        results.append(partial_tile)
    stacked = jnp.stack(results)
    return lax.psum_scatter(stacked, "aux", scatter_dimension=1, tiled=True)


def solution(mesh):
    in_specs = (P("aux", None, "basis"),)
    out_specs = P(None, ("basis", "aux"), None)
    return jax.shard_map(
        on_device, mesh=mesh, in_specs=in_specs, out_specs=out_specs, check_vma=False
    )
```

profile of v0, /device:TPU:2, one launch (start us, length us, event | category | flops | bytes accessed | tf_op | source)
XLA Modules:
  0.0 297.7 jit_solution(9849504261512879795)
XLA Ops:
  6.5 0.0 copy-start
  6.5 0.0 reduce-scatter.2.cloned.1.call-start
  6.5 2.0 collective-permute-start
  8.6 23.3 %collective-permute-done = bf16[4,500,512]{2,0,1:T(4,128)(2,1)S(1)} collective-permute-done((bf16[4,500,512]{2,0,1:T(4,128)(2,1)}, bf16[4,500,512]{2,0,1:T(4,128)(2,1)S(1)}, u32[]{:S(2)}, u32[]{:S(2)}) %collective-permute-start) | collective-permute-done | bytes 2048032 | tf_op jit(solution)/shard_map/ppermute | solution.py:12
  31.9 3.7 %collective-permute-start.1 = (bf16[4,500,512]{2,0,1:T(4,128)(2,1)S(1)}, bf16[4,500,512]{2,0,1:T(4,128)(2,1)S(1)}, u32[]{:S(2)}, u32[]{:S(2)}) collective-permute-start(bf16[4,500,512]{2,0,1:T(4,128)(2,1)S(1)} %collective-permute-done), channel_id=1, source_target_pairs={{0,15},{1,0},{2,1},{3,2},{4,3},{5,4},{6,5},{7,6},{8,7},{9,8},{10,9... | collective-permute-start | bytes 6144008 | tf_op jit(solution)/shard_map/ppermute | solution.py:12
  35.6 3.7 %fusion.8 = f32[1,512,512]{2,1,0:T(8,128)S(1)} fusion(bf16[4,500,512]{2,0,1:T(4,128)(2,1)} %param.1), kind=kOutput, calls=%fused_computation.9 | convolution fusion | flops 1048576000 | bytes 3096576 | tf_op jit(solution)/shard_map/dot_general | solution.py:17
  39.3 0.0 copy-done
  39.3 1.5 fusion.11
  40.9 17.7 %collective-permute-done.1 = bf16[4,500,512]{2,0,1:T(4,128)(2,1)S(1)} collective-permute-done((bf16[4,500,512]{2,0,1:T(4,128)(2,1)S(1)}, bf16[4,500,512]{2,0,1:T(4,128)(2,1)S(1)}, u32[]{:S(2)}, u32[]{:S(2)}) %collective-permute-start.1) | collective-permute-done | bytes 2048032 | tf_op jit(solution)/shard_map/ppermute | solution.py:12
  58.6 1.5 fusion.16
  60.1 2.0 pad_maximum_fusion
  62.1 0.0 reduce-scatter.2.cloned.1.call-update
  62.1 228.7 %reduce-scatter.2.cloned.1.call-done = f32[3,16,512]{2,1,0:T(8,128)} async-done(((f32[3,512,512]{2,1,0:T(8,128)}), f32[3,16,512]{2,1,0:T(8,128)}) %reduce-scatter.2.cloned.1.call-update) | async-done | bytes 98320 | tf_op jit(solution)/shard_map/reduce_scatter | solution.py:32
Async XLA Ops:
  6.5 32.8 %copy-start = (bf16[4,500,512]{2,0,1:T(4,128)(2,1)S(1)}, bf16[4,500,512]{2,0,1:T(4,128)(2,1)}, u32[]{:S(2)}) copy-start(bf16[4,500,512]{2,0,1:T(4,128)(2,1)} %param.1) | copy-start | bytes 6144004
  6.5 284.3 %reduce-scatter.2.cloned.1.call-start = ((), (), s32[]{:S(2)}) async-start(), calls=%async_computation.1 | async-start | bytes 3244032 | tf_op jit(solution)/shard_map/reduce_scatter | solution.py:32
  6.5 25.4 %collective-permute-start = (bf16[4,500,512]{2,0,1:T(4,128)(2,1)}, bf16[4,500,512]{2,0,1:T(4,128)(2,1)S(1)}, u32[]{:S(2)}, u32[]{:S(2)}) collective-permute-start(bf16[4,500,512]{2,0,1:T(4,128)(2,1)} %param.1), channel_id=1, source_target_pairs={{0,15},{1,0},{2,1},{3,2},{4,3},{5,4},{6,5},{7,6},{8,7},{9,8},{10,9... | collective-permute-start | bytes 6144008 | tf_op jit(solution)/shard_map/ppermute | solution.py:12
  31.9 26.7 %collective-permute-start.1 = (bf16[4,500,512]{2,0,1:T(4,128)(2,1)S(1)}, bf16[4,500,512]{2,0,1:T(4,128)(2,1)S(1)}, u32[]{:S(2)}, u32[]{:S(2)}) collective-permute-start(bf16[4,500,512]{2,0,1:T(4,128)(2,1)S(1)} %collective-permute-done), channel_id=1, source_target_pairs={{0,15},{1,0},{2,1},{3,2},{4,3},{5,4},{6,5},{7,6},{8,7},{9,8},{10,9... | collective-permute-start | bytes 6144008 | tf_op jit(solution)/shard_map/ppermute | solution.py:12
Sparse Core Ops, SparseCore 0:
  62.2 228.5 reduce-scatter.1
where the time goes:
time: 298 us
  waiting for transfers between devices  270 us (91%)
  between operations  13.4 us (4%)
  matrix products  6.75 us (2%)
  starting transfers between devices  5.74 us (2%)
    reduce_scatter x1, waiting for transfers between devices, on_device(): return lax.psum_scatter(stacked, 'aux', scatter_dimension=1, tiled=True)  229 us
    ppermute x2, waiting for transfers between devices, from_behind(): return lax.ppermute(value, axis, pairs)  41.1 us
    dot_general x3, matrix products, form_tile(): lax.dot_general(own_flat, other, (((0,), (0,)), ((), ())), preferred_elem...  6.75 us
  transfers between devices with their start and end apart: 3, of which 3 were waited for; matrix products, arithmetic and copies ran while one was open for 2% of the time, Pallas kernels for 0%

commit v1 on v0

v1 whole, which is shorter than its diff:
```python
import jax
import jax.numpy as jnp
from jax import lax
from jax.sharding import Mesh, PartitionSpec as P

SIZES = {"zl": 4, "y": 8, "zh": 2, "x": 4, "c": 2}
AUX = ("zl", "y")
BASIS = ("zh", "x", "c")


def send(value, axes, target):
    sizes = [SIZES[a] for a in axes]
    count = 1
    for size in sizes:
        count *= size

    def coords(index):
        out = []
        for size in reversed(sizes):
            out.append(index % size)
            index //= size
        return tuple(reversed(out))

    def flat(position):
        index = 0
        for size, p in zip(sizes, position):
            index = index * size + p
        return index

    pairs = []
    for i in range(count):
        to = target(*coords(i))
        if to is not None:
            pairs.append((i, flat(to)))
    return lax.ppermute(value, axes, pairs)


def along_x(zh, x, c):
    if c == 0:
        return (zh, x - 1, 0) if x > 0 else None
    return (zh, x + 1, 1) if x < 3 else None


def across_z(zh, x, c):
    if c == 0 and x == 0:
        return (1 - zh, 3, 0)
    if c == 1 and x == 3:
        return (1 - zh, 0, 1)
    return None


def to_previous_chip(zh, x, c):
    if c == 0:
        return None
    return (zh, x - 1, 1) if x > 0 else (1 - zh, 3, 1)


def other_core(c):
    return (1 - c,)


def product(a, b):
    return lax.dot_general(a, b, (((0, 1), (0, 1)), ((), ())), preferred_element_type=jnp.float32)


def code(full, half):
    top = jnp.maximum(jnp.max(jnp.abs(full)), jnp.max(jnp.abs(half)))
    power = jnp.clip(jnp.floor(jnp.log2(jnp.maximum(top, 1e-30))), -100.0, 100.0)
    scale = jnp.exp2(13.0 - power)

    def part(tile):
        cols = tile.shape[1] // 128
        tile = (tile * scale).astype(jnp.float16)
        return tile.reshape(32, 16, cols, 128).transpose(0, 2, 1, 3).reshape(32, 16 * cols, 128)

    return jnp.concatenate([part(full), part(half)], axis=1), power.astype(jnp.float16)


def add_up(parts):
    power = parts[:, -1, 0].astype(jnp.float32)
    return jnp.sum(parts[:, :-8].astype(jnp.float32) * jnp.exp2(power - 13.0)[:, None, None], axis=0)


def rows_of(cols, value):
    return value.reshape(cols, 16, 128).transpose(1, 0, 2).reshape(16, cols * 128)


def on_device(own):
    core = lax.axis_index("c")
    x = lax.axis_index("x")
    crossed = send(own, BASIS, across_z)
    beside = send(own, ("c",), other_core)
    along = send(own, BASIS, along_x)

    first = core == 0
    early_full = product(own, own)
    early_half = lax.cond(
        first,
        lambda: product(own, beside[:, :, :256]),
        lambda: product(beside, own[:, :, 256:]),
    )
    coded, power = code(early_full, early_half)
    coded = coded.reshape(4, 8, 96, 128).transpose(1, 0, 2, 3).reshape(8, 384, 128)
    coded = jnp.concatenate([coded, jnp.broadcast_to(power, (8, 8, 128))], axis=1)
    coded = lax.all_to_all(coded, "y", 0, 0, tiled=True)
    early = add_up(coded).reshape(4, 96, 128)
    early = jnp.sum(lax.all_to_all(early, "zl", 0, 0, tiled=True), axis=0)

    at_end = jnp.where(first, x == 3, x == 0)
    moved = jnp.where(at_end, crossed, along)
    late_full, late_half = lax.cond(
        first,
        lambda: (product(own, moved), product(beside, moved[:, :, :256])),
        lambda: (product(moved, own), product(moved, beside[:, :, 256:])),
    )
    coded, power = code(late_full, late_half)
    coded = jnp.concatenate([coded, jnp.broadcast_to(power, (32, 8, 128))], axis=1)
    coded = lax.all_to_all(coded, AUX, 0, 0, tiled=True)
    late = add_up(coded)

    swapped = send(jnp.where(first, late[64:], early[64:]), ("c",), other_core)
    back = send(late, BASIS, to_previous_chip)

    s0 = rows_of(4, early[:64])
    s1 = rows_of(4, jnp.where(first, jnp.concatenate([early[64:], swapped]), jnp.concatenate([swapped, back[64:]])))
    s2 = rows_of(4, jnp.where(first, late[:64], back[:64]))
    return jnp.stack([s0, s1, s2])


def solution(mesh):
    fine = Mesh(mesh.devices.reshape(tuple(SIZES.values())), tuple(SIZES))
    return jax.shard_map(
        on_device, mesh=fine, in_specs=(P(AUX, None, BASIS),), out_specs=P(None, BASIS + AUX, None), check_vma=False
    )
```

time: 298 us -> 124 us (0.42)
  the two profiles are of different devices: /device:TPU:2 before, /device:TPU:9 now
where the time goes in v1:
time: 124 us; the launch traced here: 123 us
  starting transfers between devices  58.7 us (47%)
  waiting for transfers between devices  34.8 us (28%)
  matrix products  12.9 us (10%)
  other arithmetic  7.22 us (6%)
  local copies, waits for them, and re-layouts  5.99 us (5%)
  loops' own time  1.67 us (1%)
  between operations  1.62 us (1%)
    all_to_all x1, starting transfers between devices, on_device(): coded = lax.all_to_all(coded, AUX, 0, 0, tiled=True)  30.9 us
    all_to_all x1, waiting for transfers between devices, on_device(): coded = lax.all_to_all(coded, AUX, 0, 0, tiled=True)  22.9 us
    ppermute x5, starting transfers between devices, send(): return lax.ppermute(value, axes, pairs)  17.5 us
    dot_general x4, matrix products, product(): lax.dot_general(a, b, (((0, 1), (0, 1)), ((), ())), preferred_element_typ...  12.9 us
    ppermute x5, waiting for transfers between devices, send(): return lax.ppermute(value, axes, pairs)  9.06 us
    all_to_all x1, starting transfers between devices, on_device(): coded = lax.all_to_all(coded, 'y', 0, 0, tiled=True)  6.98 us
    all_to_all x1, starting transfers between devices, on_device(): early = jnp.sum(lax.all_to_all(early, 'zl', 0, 0, tiled=True), axis=0)  3.36 us
    all_to_all x1, waiting for transfers between devices, on_device(): early = jnp.sum(lax.all_to_all(early, 'zl', 0, 0, tiled=True), axis=0)  2.81 us
  transfers between devices with their start and end apart: 8, of which 4 were waited for; matrix products, arithmetic and copies ran while one was open for 20% of the time, Pallas kernels for 0%

profile of v1, /device:TPU:9, one launch (start us, length us, event | category | flops | bytes accessed | tf_op | source)
XLA Modules:
  0.0 122.9 jit_solution(7818627188343821968)
XLA Ops:
  0.0 2.6 %collective-permute-start = (bf16[4,500,512]{2,0,1:T(4,128)(2,1)}, bf16[4,500,512]{2,0,1:T(4,128)(2,1)}, u32[]{:S(2)}, u32[]{:S(2)}) collective-permute-start(bf16[4,500,512]{2,0,1:T(4,128)(2,1)} %param.5), channel_id=1, source_target_pairs={{0,1},{1,0},{2,3},{3,2},{4,5},{5,4},{6,7},{7,6},{8,9},{9,8},{10,11... | collective-permute-start | bytes 6144008 | tf_op jit(solution)/shard_map/ppermute | solution.py:35
  2.6 1.3 %collective-permute-start.1 = (bf16[4,500,512]{2,0,1:T(4,128)(2,1)}, bf16[4,500,512]{2,0,1:T(4,128)(2,1)}, u32[]{:S(2)}, u32[]{:S(2)}) collective-permute-start(bf16[4,500,512]{2,0,1:T(4,128)(2,1)} %param.5), channel_id=1, source_target_pairs={{0,14},{7,9},{8,6},{15,1},{16,30},{23,25},{24,22},{31,17},{32,46},... | collective-permute-start | bytes 6144008 | tf_op jit(solution)/shard_map/ppermute | solution.py:35
  3.9 5.1 %collective-permute-start.2 = (bf16[4,500,512]{2,0,1:T(4,128)(2,1)}, bf16[4,500,512]{2,0,1:T(4,128)(2,1)}, u32[]{:S(2)}, u32[]{:S(2)}) collective-permute-start(bf16[4,500,512]{2,0,1:T(4,128)(2,1)} %param.5), channel_id=1, source_target_pairs={{1,3},{2,0},{3,5},{4,2},{5,7},{6,4},{9,11},{10,8},{11,13},{12,10},... | collective-permute-start | bytes 6144008 | tf_op jit(solution)/shard_map/ppermute | solution.py:35
  9.0 5.5 %abs_reduce_fusion.4 = (f32[]{:T(128)}, f32[512,512]{1,0:T(8,128)}) fusion(bf16[4,500,512]{2,0,1:T(4,128)(2,1)} %param.5), kind=kOutput, calls=%fused_computation.36 | convolution fusion | flops 1049100288 | bytes 3096580 | tf_op jit(solution)/shard_map/dot_general | solution.py:63
  14.5 0.0 collective-permute-done
  14.5 0.0 copy-done
  14.5 3.0 %conditional.2 = (f32[512,256]{1,0:T(8,128)S(1)}) conditional(s32[]{:T(128)} %convert_element_type.36, (bf16[4,500,512]{2,0,1:T(4,128)(2,1)S(1)}, bf16[4,500,512]{2,0,1:T(4,128)(2,1)}) %tuple.130, (bf16[4,500,512]{2,0,1:T(4,128)(2,1)}, bf16[4,500,512]{2,0,1:T(4,128)(2,1)S(1)}) %tuple.131), branch_computations={%region_1.0_spmd, %region_2.0_spmd} | conditional | flops 524288000 | bytes 7700488 | solution.py:97
  14.5 0.4 copy.143
  14.9 2.6 %fusion.2 = f32[512,256]{1,0:T(8,128)S(1)} fusion(bf16[4,500,512]{2,0,1:T(4,128)(2,1)} %get-tuple-element.216, bf16[4,500,512]{2,1,0:T(8,128)(2,1)S(1)} %copy.143), kind=kOutput, calls=%fused_computation.2 | convolution fusion | flops 524288000 | bytes 3604480 | tf_op jit(solution)/shard_map/cond/branch_0_fun/dot_general | solution.py:63
  17.5 0.6 abs_reduce_fusion.5
  19.4 0.1 reshape.43
  19.5 0.1 copy.148
  19.6 1.4 %multiply_convert_fusion.1 = f16[512,512]{1,0:T(8,128)(2,1)S(1)} fusion(f32[512,512]{1,0:T(8,128)} %get-tuple-element.253, f32[]{:T(128)S(6)} %exp2.42), kind=kLoop, calls=%fused_computation.35 | loop fusion | flops 524288 | bytes 1572868 | tf_op jit(solution)/shard_map/convert_element_type | solution.py:73
  21.0 0.2 reshape.42
  21.2 0.2 copy.147
  21.3 0.2 maximum_bitcast_fusion
  21.5 0.2 copy.149
  21.7 1.1 concatenate.23
  22.8 7.0 %all-to-all-start = ((f16[8,392,128]{2,1,0:T(8,128)(2,1)}), f16[8,392,128]{2,1,0:T(8,128)(2,1)S(1)}, u32[]{:S(2)}, u32[]{:S(2)}) async-start(f16[8,392,128]{2,1,0:T(8,128)(2,1)} %concatenate.23), calls=%async_computation | async-start | bytes 1605632 | tf_op jit(solution)/shard_map/all_to_all | solution.py:105
  29.8 8.4 %collective-permute-done.1 = bf16[4,500,512]{2,0,1:T(4,128)(2,1)} collective-permute-done((bf16[4,500,512]{2,0,1:T(4,128)(2,1)}, bf16[4,500,512]{2,0,1:T(4,128)(2,1)}, u32[]{:S(2)}, u32[]{:S(2)}) %collective-permute-start.1) | collective-permute-done | bytes 2048032 | tf_op jit(solution)/shard_map/ppermute | solution.py:35
  38.1 0.0 collective-permute-done.2
  38.1 1.8 %broadcast_select_fusion = bf16[8,250,512]{2,0,1:T(8,128)(2,1)S(1)} fusion(bf16[8,250,512]{2,0,1:T(8,128)(2,1)} %bitcast.46, bf16[8,250,512]{2,0,1:T(8,128)(2,1)} %bitcast.47, pred[]{:T(512)S(6)} %select_n.38), kind=kLoop, calls=%fused_computation.30 | loop fusion | flops 1024000 | bytes 6144001 | tf_op jit(solution)/shard_map/jit(_where)/select_n | solution.py:110
  39.9 8.4 %conditional.3 = (f32[512,512]{1,0:T(8,128)}, f32[512,256]{1,0:T(8,128)S(1)}, f32[]{:T(128)}, f32[]{:T(128)}) conditional(s32[]{:T(128)} %convert_element_type.36, (bf16[4,500,512]{2,0,1:T(4,128)(2,1)S(1)}, bf16[4,500,512]{2,0,1:T(4,128)(2,1)S(1)}, bf16[4,500,512]{2,0,1:T(4,128)(2,1)}) %tuple.132, ...), branch_computations={%region_6.7_spmd.clone.clone, %region_7.8_spmd.clone.clone} | conditional | flops 1573650432 | bytes 12845204 | solution.py:111
  39.9 3.1 %abs_reduce_fusion = (f32[]{:T(128)}, f32[512,512]{1,0:T(8,128)}) fusion(bf16[4,500,512]{2,0,1:T(4,128)(2,1)S(1)} %get-tuple-element.229, bf16[4,500,512]{2,0,1:T(4,128)(2,1)S(1)} %get-tuple-element.228), kind=kOutput, calls=%fused_computation.15 | convolution fusion | flops 1049100288 | bytes 5144580 | tf_op jit(solution)/shard_map/cond/branch_0_fun/dot_general | solution.py:63
  43.1 2.0 %copy.165 = bf16[4,500,512]{2,1,0:T(8,128)(2,1)S(1)} copy(bf16[4,500,512]{2,0,1:T(4,128)(2,1)} %get-tuple-element.230) | data formatting | bytes 4096000 | tf_op jit(solution)/shard_map
  45.1 1.7 %abs_reduce_fusion.1 = (f32[]{:T(128)}, f32[512,256]{1,0:T(8,128)S(1)}) fusion(bf16[4,500,512]{2,1,0:T(8,128)(2,1)S(1)} %copy.165, bf16[4,500,512]{2,0,1:T(4,128)(2,1)S(1)} %get-tuple-element.228), kind=kOutput, calls=%fused_computation.17 | convolution fusion | flops 524550144 | bytes 3604484 | tf_op jit(solution)/shard_map/cond/branch_0_fun/dot_general | solution.py:63
  48.4 0.1 reshape.49
  48.5 0.1 copy.159
  48.6 1.0 copy-done.1
  49.6 0.1 multiply_convert_fusion
  49.7 0.2 reshape.47
  49.9 0.2 copy.158
  50.1 0.1 pad.10.clone
  50.2 1.2 maximum_maximum_fusion
  51.4 0.0 all-to-all-done
  51.4 30.9 %all-to-all-start.2 = ((f16[32,104,128]{2,1,0:T(8,128)(2,1)}), f16[32,104,128]{2,1,0:T(8,128)(2,1)S(1)}, u32[]{:S(2)}, u32[]{:S(2)}) async-start(f16[32,104,128]{2,1,0:T(8,128)(2,1)} %maximum_maximum_fusion), calls=%async_computation.2 | async-start | bytes 1703936 | tf_op jit(solution)/shard_map/all_to_all | solution.py:118
  82.3 0.1 copy.169
  82.4 0.9 multiply_reduce_fusion.1
  83.3 22.9 %all-to-all-done.2 = f16[32,104,128]{2,1,0:T(8,128)(2,1)S(1)} async-done(((f16[32,104,128]{2,1,0:T(8,128)(2,1)}), f16[32,104,128]{2,1,0:T(8,128)(2,1)S(1)}, u32[]{:S(2)}, u32[]{:S(2)}) %all-to-all-start.2) | async-done | bytes 852000 | tf_op jit(solution)/shard_map/all_to_all | solution.py:118
  106.3 3.4 %all-to-all-start.1 = ((f32[4,96,128]{2,1,0:T(8,128)}), f32[4,96,128]{2,1,0:T(8,128)S(1)}, u32[]{:S(2)}, u32[]{:S(2)}) async-start(f32[4,96,128]{2,1,0:T(8,128)} %bitcast.10), calls=%async_computation.1 | async-start | bytes 393216 | tf_op jit(solution)/shard_map/all_to_all | solution.py:107
  109.7 0.1 copy.170
  109.8 0.2 multiply_reduce_fusion
  110.0 1.9 %collective-permute-start.4 = (f32[96,128]{1,0:T(8,128)S(1)}, f32[96,128]{1,0:T(8,128)S(1)}, u32[]{:S(2)}, u32[]{:S(2)}) collective-permute-start(f32[96,128]{1,0:T(8,128)S(1)} %multiply_reduce_fusion), channel_id=1, source_target_pairs={{1,15},{3,1},{5,3},{7,5},{9,7},{11,9},{13,11},{15,13},{17,31},{19,... | collective-permute-start | bytes 147464 | tf_op jit(solution)/shard_map/ppermute | solution.py:35
  111.9 2.8 %all-to-all-done.1 = f32[4,96,128]{2,1,0:T(8,128)S(1)} async-done(((f32[4,96,128]{2,1,0:T(8,128)}), f32[4,96,128]{2,1,0:T(8,128)S(1)}, u32[]{:S(2)}, u32[]{:S(2)}) %all-to-all-start.1) | async-done | bytes 196640 | tf_op jit(solution)/shard_map/all_to_all | solution.py:107
  114.8 6.6 %collective-permute-start.3 = (f32[32,128]{1,0:T(8,128)S(1)}, f32[32,128]{1,0:T(8,128)S(1)}, u32[]{:S(2)}, u32[]{:S(2)}) collective-permute-start(f32[32,128]{1,0:T(8,128)S(1)} %get-tuple-element.251), channel_id=1, source_target_pairs={{0,1},{1,0},{2,3},{3,2},{4,5},{5,4},{6,7},{7,6},{8,9},{9,8},{10,11... | collective-permute-start | bytes 49160 | tf_op jit(solution)/shard_map/ppermute | solution.py:35
  121.4 0.0 collective-permute-done.4
  121.5 0.7 collective-permute-done.3
  122.3 0.6 pad_maximum_fusion
  (21 shorter events, 0.3 us)
Async XLA Ops:
  0.0 14.5 %collective-permute-start = (bf16[4,500,512]{2,0,1:T(4,128)(2,1)}, bf16[4,500,512]{2,0,1:T(4,128)(2,1)}, u32[]{:S(2)}, u32[]{:S(2)}) collective-permute-start(bf16[4,500,512]{2,0,1:T(4,128)(2,1)} %param.5), channel_id=1, source_target_pairs={{0,1},{1,0},{2,3},{3,2},{4,5},{5,4},{6,7},{7,6},{8,9},{9,8},{10,11... | collective-permute-start | bytes 6144008 | tf_op jit(solution)/shard_map/ppermute | solution.py:35
  2.6 35.6 %collective-permute-start.1 = (bf16[4,500,512]{2,0,1:T(4,128)(2,1)}, bf16[4,500,512]{2,0,1:T(4,128)(2,1)}, u32[]{:S(2)}, u32[]{:S(2)}) collective-permute-start(bf16[4,500,512]{2,0,1:T(4,128)(2,1)} %param.5), channel_id=1, source_target_pairs={{0,14},{7,9},{8,6},{15,1},{16,30},{23,25},{24,22},{31,17},{32,46},... | collective-permute-start | bytes 6144008 | tf_op jit(solution)/shard_map/ppermute | solution.py:35
  3.9 34.3 %collective-permute-start.2 = (bf16[4,500,512]{2,0,1:T(4,128)(2,1)}, bf16[4,500,512]{2,0,1:T(4,128)(2,1)}, u32[]{:S(2)}, u32[]{:S(2)}) collective-permute-start(bf16[4,500,512]{2,0,1:T(4,128)(2,1)} %param.5), channel_id=1, source_target_pairs={{1,3},{2,0},{3,5},{4,2},{5,7},{6,4},{9,11},{10,8},{11,13},{12,10},... | collective-permute-start | bytes 6144008 | tf_op jit(solution)/shard_map/ppermute | solution.py:35
  9.0 5.5 %copy-start = (bf16[4,500,512]{2,0,1:T(4,128)(2,1)S(1)}, bf16[4,500,512]{2,0,1:T(4,128)(2,1)}, u32[]{:S(2)}) copy-start(bf16[4,500,512]{2,0,1:T(4,128)(2,1)} %param.5) | copy-start | bytes 6144004
  22.8 28.6 %all-to-all-start = ((f16[8,392,128]{2,1,0:T(8,128)(2,1)}), f16[8,392,128]{2,1,0:T(8,128)(2,1)S(1)}, u32[]{:S(2)}, u32[]{:S(2)}) async-start(f16[8,392,128]{2,1,0:T(8,128)(2,1)} %concatenate.23), calls=%async_computation | async-start | bytes 1605632 | tf_op jit(solution)/shard_map/all_to_all | solution.py:105
  48.4 1.2 copy-start.1
  51.4 54.9 %all-to-all-start.2 = ((f16[32,104,128]{2,1,0:T(8,128)(2,1)}), f16[32,104,128]{2,1,0:T(8,128)(2,1)S(1)}, u32[]{:S(2)}, u32[]{:S(2)}) async-start(f16[32,104,128]{2,1,0:T(8,128)(2,1)} %maximum_maximum_fusion), calls=%async_computation.2 | async-start | bytes 1703936 | tf_op jit(solution)/shard_map/all_to_all | solution.py:118
  106.3 8.5 %all-to-all-start.1 = ((f32[4,96,128]{2,1,0:T(8,128)}), f32[4,96,128]{2,1,0:T(8,128)S(1)}, u32[]{:S(2)}, u32[]{:S(2)}) async-start(f32[4,96,128]{2,1,0:T(8,128)} %bitcast.10), calls=%async_computation.1 | async-start | bytes 393216 | tf_op jit(solution)/shard_map/all_to_all | solution.py:107
  110.0 11.4 %collective-permute-start.4 = (f32[96,128]{1,0:T(8,128)S(1)}, f32[96,128]{1,0:T(8,128)S(1)}, u32[]{:S(2)}, u32[]{:S(2)}) collective-permute-start(f32[96,128]{1,0:T(8,128)S(1)} %multiply_reduce_fusion), channel_id=1, source_target_pairs={{1,15},{3,1},{5,3},{7,5},{9,7},{11,9},{13,11},{15,13},{17,31},{19,... | collective-permute-start | bytes 147464 | tf_op jit(solution)/shard_map/ppermute | solution.py:35
  114.8 7.4 %collective-permute-start.3 = (f32[32,128]{1,0:T(8,128)S(1)}, f32[32,128]{1,0:T(8,128)S(1)}, u32[]{:S(2)}, u32[]{:S(2)}) collective-permute-start(f32[32,128]{1,0:T(8,128)S(1)} %get-tuple-element.251), channel_id=1, source_target_pairs={{0,1},{1,0},{2,3},{3,2},{4,5},{5,4},{6,7},{7,6},{8,9},{9,8},{10,11... | collective-permute-start | bytes 49160 | tf_op jit(solution)/shard_map/ppermute | solution.py:35

commit v2 on v1

v2 whole, which is shorter than its diff:
```python
import functools

import jax
import jax.numpy as jnp
from jax import lax
from jax.experimental import pallas as pl
from jax.experimental.pallas import tpu as pltpu
from jax.sharding import Mesh, PartitionSpec as P

SIZES = {"zl": 4, "y": 8, "zh": 2, "x": 4, "c": 2}
AUX = ("zl", "y")
BASIS = ("zh", "x", "c")


def send(value, axes, target):
    sizes = [SIZES[a] for a in axes]
    count = 1
    for size in sizes:
        count *= size

    def coords(index):
        out = []
        for size in reversed(sizes):
            out.append(index % size)
            index //= size
        return tuple(reversed(out))

    def flat(position):
        index = 0
        for size, p in zip(sizes, position):
            index = index * size + p
        return index

    pairs = []
    for i in range(count):
        to = target(*coords(i))
        if to is not None:
            pairs.append((i, flat(to)))
    return lax.ppermute(value, axes, pairs)


def along_x(zh, x, c):
    if c == 0:
        return (zh, x - 1, 0) if x > 0 else None
    return (zh, x + 1, 1) if x < 3 else None


def across_z(zh, x, c):
    if c == 0 and x == 0:
        return (1 - zh, 3, 0)
    if c == 1 and x == 3:
        return (1 - zh, 0, 1)
    return None


def to_previous_chip(zh, x, c):
    if c == 0:
        return None
    return (zh, x - 1, 1) if x > 0 else (1 - zh, 3, 1)


def other_core(c):
    return (1 - c,)


def product(a, b):
    return lax.dot_general(a, b, (((0,), (0,)), ((), ())), preferred_element_type=jnp.float32)


def columns(ref, low=0, high=512):
    return ref[:, :, low:high].reshape(-1, high - low)


def put(out, full, half, place):
    base = 0
    top = jnp.zeros((8, 128), jnp.float32)
    for tile in (full, half):
        cols = tile.shape[1] // 128
        for owner in range(32):
            for r in range(2):
                rows = tile[owner * 16 + r * 8 : owner * 16 + r * 8 + 8]
                for c in range(cols):
                    piece = rows[:, c * 128 : c * 128 + 128]
                    row = base + (r * cols + c) * 8
                    lead, at = place(owner, row)
                    if place(owner, row + 4) == (lead, at + 4):
                        out[lead, at : at + 8, :] = piece
                    else:
                        out[lead, at : at + 4, :] = piece[:4]
                        lead, at = place(owner, row + 4)
                        out[lead, at : at + 4, :] = piece[4:]
                    top = jnp.maximum(top, jnp.abs(piece))
        base += 16 * cols
    return top


def power_of(top):
    top = jnp.max(top, axis=(0, 1), keepdims=True)
    return jnp.clip(jnp.floor(jnp.log2(jnp.maximum(top, 1e-30))), -100.0, 100.0)


def scale_down(out, rows, power):
    out[:, :rows, :] = out[:, :rows, :] * jnp.exp2(13.0 - power)[None]
    out[:, rows : rows + 8, :] = jnp.broadcast_to(power[None], (out.shape[0], 8, 128))


def by_owner(owner, row):
    return owner % 8, owner // 8 * 96 + row


def by_slice(owner, row):
    return row // 12, owner * 12 + row % 12


def by_device(owner, row):
    return owner, row


def early_kernel(flags, own, beside, out, top):
    def form(rows, cols, low, place):
        full = product(columns(own), columns(own))
        half = product(columns(rows), columns(cols, low, low + 256))
        top[...] = put(out, full, half, place)

    for core, blocks in ((0, (own, beside, 0)), (1, (beside, own, 256))):
        for end, place in ((0, by_owner), (1, by_slice)):
            pl.when((flags[0] == core) & (flags[1] == end))(functools.partial(form, *blocks, place))
    scale_down(out, 384, power_of(top[...]))


def late_kernel(place, flags, own, beside, moved, early, out, top, own_here, beside_here, moved_here, arrived):
    cuts = (0, 250, 500)

    def fetch(k, n, source, target):
        rows = pl.ds(cuts[k], cuts[k + 1] - cuts[k])
        return pltpu.make_async_copy(source.at[rows], target.at[rows], arrived.at[k, n])

    for k in (0, 1):
        fetch(k, 0, own, own_here).start()
        fetch(k, 1, moved, moved_here).start()
        fetch(k, 2, beside, beside_here).start()

    def form(core):
        full = half = 0.0
        for k in (0, 1):
            rows = slice(cuts[k], cuts[k + 1])
            fetch(k, 0, own, own_here).wait()
            fetch(k, 1, moved, moved_here).wait()
            mine, other = columns(own_here.at[rows]), columns(moved_here.at[rows])
            full += product(mine, other) if core == 0 else product(other, mine)
            fetch(k, 2, beside, beside_here).wait()
            if core == 0:
                half += product(columns(beside_here.at[rows]), columns(moved_here.at[rows], 0, 256))
            else:
                half += product(columns(moved_here.at[rows]), columns(beside_here.at[rows], 256, 512))
        top[...] = put(out, full, half, place)

    for core in (0, 1):
        pl.when(flags[0] == core)(functools.partial(form, core))
    if place is by_owner:
        scale_down(out, 384, power_of(top[...]))
        return
    scale_down(out, 96, power_of(top[...]))
    sums = early[...]
    power = power_of(jnp.abs(sums))
    sums = sums * jnp.exp2(13.0 - power)
    for owner in range(32):
        out[owner, 104:116, :] = sums[owner * 12 : owner * 12 + 12]
    out[:, 116:, :] = jnp.broadcast_to(power[None], (32, 4, 128))


def call(kernel, shape, flags, *blocks, early=None):
    vmem = pl.BlockSpec(memory_space=pltpu.VMEM)
    blocks = [block.transpose(1, 0, 2) for block in blocks]
    specs = [vmem] * len(blocks)
    scratch = [pltpu.VMEM((8, 128), jnp.float32)]
    if early is not None:
        specs = [pl.BlockSpec(memory_space=pl.ANY)] * len(blocks) + [vmem]
        scratch += [pltpu.VMEM(blocks[0].shape, jnp.bfloat16)] * 3 + [pltpu.SemaphoreType.DMA((2, 3))]
        blocks.append(early)
    return pl.pallas_call(
        kernel,
        out_shape=jax.ShapeDtypeStruct(shape, jnp.float32),
        in_specs=[pl.BlockSpec(memory_space=pltpu.SMEM)] + specs,
        out_specs=vmem,
        scratch_shapes=scratch,
        compiler_params=pltpu.CompilerParams(vmem_limit_bytes=40 << 20),
        cost_estimate=pl.CostEstimate(flops=1_600_000_000, bytes_accessed=8_000_000, transcendentals=0),
    )(flags, *blocks).astype(jnp.float16)


def untiled(value, cols):
    return value.reshape(2, cols // 128, 8, 128).transpose(0, 2, 1, 3).reshape(16, cols)


def unscaled(parts, power):
    return parts.astype(jnp.float32) * jnp.exp2(power.astype(jnp.float32) - 13.0)[:, None, None]


def on_device(own):
    core = lax.axis_index("c")
    x = lax.axis_index("x")
    first = core == 0
    at_end = jnp.where(first, x == 3, x == 0)
    flags = jnp.stack([core, at_end.astype(jnp.int32)])

    crossed = send(own, BASIS, across_z)
    beside = send(own, ("c",), other_core)
    along = send(own, BASIS, along_x)

    def add_over_y(parts):
        parts = lax.all_to_all(parts, "y", 0, 0, tiled=True)
        return jnp.sum(unscaled(parts[:, :384], parts[:, -1, 0]), axis=0)

    def form_early():
        return add_over_y(call(early_kernel, (8, 392, 128), flags, own, beside))

    def late_over_y():
        kernel = functools.partial(late_kernel, by_owner)
        return add_over_y(call(kernel, (8, 392, 128), flags, own, beside, along, early=total))

    def over_z():
        parts = jnp.concatenate([total.reshape(4, 96, 128), late_total.reshape(4, 96, 128)], axis=1)
        parts = jnp.sum(lax.all_to_all(parts, "zl", 0, 0, tiled=True), axis=0)
        return parts[:96], parts[96:]

    def late_over_aux():
        kernel = functools.partial(late_kernel, by_device)
        parts = call(kernel, (32, 120, 128), flags, own, beside, crossed, early=total)
        parts = lax.all_to_all(parts, AUX, 0, 0, tiled=True)
        late = jnp.sum(unscaled(parts[:, :96], parts[:, 103, 0]), axis=0)
        early = unscaled(parts[:, 104:116], parts[:, 119, 0]).reshape(4, 8, 12, 128)
        return jnp.sum(early, axis=0).reshape(96, 128), late

    nothing = lambda: jnp.zeros((384, 128), jnp.float32)
    total = lax.cond(core < 2, form_early, nothing)
    total, along = lax.optimization_barrier((total, along))
    late_total = lax.cond(at_end, nothing, late_over_y)
    late_total, crossed = lax.optimization_barrier((late_total, crossed))
    early, late = lax.cond(at_end, late_over_aux, over_z)

    swapped = send(jnp.where(first, late[64:], early[64:]), ("c",), other_core)
    back = send(late, BASIS, to_previous_chip)

    s0 = untiled(early[:64], 512)
    left = untiled(jnp.where(first, early[64:], swapped), 256)
    right = untiled(jnp.where(first, swapped, back[64:]), 256)
    s1 = jnp.concatenate([left, right], axis=1)
    s2 = untiled(jnp.where(first, late[:64], back[:64]), 512)
    return jnp.stack([s0, s1, s2])


def solution(mesh):
    fine = Mesh(mesh.devices.reshape(tuple(SIZES.values())), tuple(SIZES))
    return jax.shard_map(
        on_device, mesh=fine, in_specs=(P(AUX, None, BASIS),), out_specs=P(None, BASIS + AUX, None), check_vma=False
    )
```

time: 124 us -> 110 us (0.89)
  the two profiles are of different devices: /device:TPU:9 before, /device:TPU:15 now
where the time goes in v2:
time: 110 us; the launch traced here: 109 us
  blocking collectives  51.7 us (47%)
  starting transfers between devices  38.2 us (35%)
  Pallas kernels  9.98 us (9%)
  waiting for transfers between devices  6.37 us (6%)
  other arithmetic  1.78 us (2%)
    all_to_all x2, blocking collectives, add_over_y(): parts = lax.all_to_all(parts, 'y', 0, 0, tiled=True)  38.3 us
    ppermute x5, starting transfers between devices, send(): return lax.ppermute(value, axes, pairs)  38.2 us
    all_to_all x1, blocking collectives, over_z(): parts = jnp.sum(lax.all_to_all(parts, 'zl', 0, 0, tiled=True), axis=0)  13.4 us
    pallas_call x2, Pallas kernels, call(): pl.pallas_call(kernel, out_shape=jax.ShapeDtypeStruct(shape, jnp.float32)...  9.98 us
    ppermute x5, waiting for transfers between devices, send(): return lax.ppermute(value, axes, pairs)  6.37 us
  transfers between devices with their start and end apart: 5, of which 2 were waited for; matrix products, arithmetic and copies ran while one was open for 1% of the time, Pallas kernels for 9%

profile of v2, /device:TPU:15, one launch (start us, length us, event | category | flops | bytes accessed | tf_op | source)
XLA Modules:
  0.0 109.1 jit_solution(31995978128246603)
XLA Ops:
  0.0 2.6 %collective-permute-start = (bf16[4,500,512]{2,0,1:T(4,128)(2,1)}, bf16[4,500,512]{2,0,1:T(4,128)(2,1)S(1)}, u32[]{:S(2)}, u32[]{:S(2)}) collective-permute-start(bf16[4,500,512]{2,0,1:T(4,128)(2,1)} %param.7), channel_id=1, source_target_pairs={{0,1},{1,0},{2,3},{3,2},{4,5},{5,4},{6,7},{7,6},{8,9},{9,8},{10,11... | collective-permute-start | bytes 6144008 | tf_op jit(solution)/shard_map/ppermute | solution.py:39
  2.6 1.3 %collective-permute-start.1 = (bf16[4,500,512]{2,0,1:T(4,128)(2,1)}, bf16[4,500,512]{2,0,1:T(4,128)(2,1)}, u32[]{:S(2)}, u32[]{:S(2)}) collective-permute-start(bf16[4,500,512]{2,0,1:T(4,128)(2,1)} %param.7), channel_id=1, source_target_pairs={{1,3},{2,0},{3,5},{4,2},{5,7},{6,4},{9,11},{10,8},{11,13},{12,10},... | collective-permute-start | bytes 6144008 | tf_op jit(solution)/shard_map/ppermute | solution.py:39
  3.9 15.0 %collective-permute-start.2 = (bf16[4,500,512]{2,0,1:T(4,128)(2,1)}, bf16[4,500,512]{2,0,1:T(4,128)(2,1)}, u32[]{:S(2)}, u32[]{:S(2)}) collective-permute-start(bf16[4,500,512]{2,0,1:T(4,128)(2,1)} %param.7), channel_id=1, source_target_pairs={{0,14},{7,9},{8,6},{15,1},{16,30},{23,25},{24,22},{31,17},{32,46},... | collective-permute-start | bytes 6144008 | tf_op jit(solution)/shard_map/ppermute | solution.py:39
  18.9 0.1 pad_add_fusion
  18.9 0.0 collective-permute-done
  18.9 25.0 %conditional.3 = (f32[384,128]{1,0:T(8,128)S(1)}) conditional(s32[]{:T(128)} %convert_element_type.46, () %tuple.29, (bf16[4,500,512]{2,0,1:T(4,128)(2,1)}, bf16[4,500,512]{2,0,1:T(4,128)(2,1)S(1)}, s32[2]{0:T(128)S(1)}) %tuple.30), branch_computations={%region_0.1_spmd, %region_1.3_spmd} | conditional | flops 1601531904 | bytes 12997208 | solution.py:236
  18.9 3.8 %branch_1_fun.2 = f32[8,392,128]{2,1,0:T(8,128)S(1)} custom-call(s32[2]{0:T(128)S(1)} %get-tuple-element.43.flags, bf16[500,4,512]{2,1,0:T(4,128)(2,1)} %bitcast.35, bf16[500,4,512]{2,1,0:T(4,128)(2,1)S(1)} %bitcast.38), custom_call_target="tpu_custom_call" | custom-call | flops 1600000000 | bytes 8000000 | tf_op jit(solution)/shard_map/cond/branch_1_fun/pallas_call | solution.py:181
  22.7 0.1 convert_element_type.32
  22.8 20.7 %all_to_all.16 = f16[8,392,128]{2,1,0:T(8,128)(2,1)S(1)} all-to-all(f16[8,392,128]{2,1,0:T(8,128)(2,1)S(1)} %convert_element_type.32), channel_id=1, replica_groups=mesh['zl'=4,'y'=8,'zh'=2,'x'=4,'c'=2] {'y'}, dimensions={0} | all-to-all | bytes 1605632 | tf_op jit(solution)/shard_map/cond/branch_1_fun/all_to_all | solution.py:212
  43.5 0.2 fusion.3
  43.7 0.2 multiply_reduce_fusion
  43.9 0.0 collective-permute-done.1
  43.9 24.5 %conditional.4 = (f32[384,128]{1,0:T(8,128)S(1)}) conditional(s32[]{:T(128)} %convert_element_type.45, (bf16[4,500,512]{2,0,1:T(4,128)(2,1)}, bf16[4,500,512]{2,0,1:T(4,128)(2,1)S(1)}, bf16[4,500,512]{2,0,1:T(4,128)(2,1)}, s32[2]{0:T(128)S(1)}, f32[384,128]{1,0:T(8,128)S(1)}) %tuple.32, () %tuple.33), branch_computations={%region_3.5_spmd, %region_5.6_spmd} | conditional | flops 1601531904 | bytes 12997208 | solution.py:238
  43.9 6.2 %branch_0_fun.1 = f32[8,392,128]{2,1,0:T(8,128)S(1)} custom-call(s32[2]{0:T(128)S(1)} %get-tuple-element.46.flags, bf16[500,4,512]{2,1,0:T(4,128)(2,1)} %bitcast.36, bf16[500,4,512]{2,1,0:T(4,128)(2,1)S(1)} %bitcast.39, bf16[500,4,512]{2,1,0:T(4,128)(2,1)} %bitcast.4.moved, f32[384,128]{1,0:T(8,128)S(1)} %get-tuple-element.50.early), custom_call_target="tpu_custom_call" | custom-call | flops 1600000000 | bytes 8000000 | tf_op jit(solution)/shard_map/cond/branch_0_fun/pallas_call | solution.py:181
  50.2 0.1 convert_element_type.35
  50.3 17.6 %all_to_all.17 = f16[8,392,128]{2,1,0:T(8,128)(2,1)S(1)} all-to-all(f16[8,392,128]{2,1,0:T(8,128)(2,1)S(1)} %convert_element_type.35), channel_id=1, replica_groups=mesh['zl'=4,'y'=8,'zh'=2,'x'=4,'c'=2] {'y'}, dimensions={0} | all-to-all | bytes 1605632 | tf_op jit(solution)/shard_map/cond/branch_0_fun/all_to_all | solution.py:212
  67.9 0.2 fusion.7
  68.0 0.2 multiply_reduce_fusion.1
  68.5 0.0 collective-permute-done.2
  68.5 14.2 %conditional.5 = (f32[96,128]{1,0:T(8,128)S(1)}, f32[96,128]{1,0:T(8,128)}, f32[32,128]{1,0:T(8,128)S(1)}, f32[64,128]{1,0:T(8,128)S(1)}) conditional(s32[]{:T(128)} %convert_element_type.45, (f32[384,128]{1,0:T(8,128)S(1)}, f32[384,128]{1,0:T(8,128)S(1)}) %tuple.35, (bf16[4,500,512]{2,0,1:T(4,128)(2,1)}, bf16[4,500,512]{2,0,1:T(4,128)(2,1)S(1)}, ...), branch_computations={%region_6.8_spmd, %region_8.11_spmd} | conditional | flops 1601794304 | bytes 14488740 | solution.py:240
  68.5 13.4 %all_to_all.18 = f32[4,192,128]{2,1,0:T(8,128)S(1)} all-to-all(f32[4,192,128]{2,1,0:T(8,128)S(1)} %pad_maximum_fusion), channel_id=1, replica_groups=mesh['zl'=4,'y'=8,'zh'=2,'x'=4,'c'=2] {'zl'}, dimensions={0} | all-to-all | bytes 786432 | tf_op jit(solution)/shard_map/cond/branch_0_fun/all_to_all | solution.py:224
  82.0 0.6 fusion.16
  82.6 7.0 %collective-permute-start.4 = (f32[96,128]{1,0:T(8,128)}, f32[96,128]{1,0:T(8,128)S(1)}, u32[]{:S(2)}, u32[]{:S(2)}) collective-permute-start(f32[96,128]{1,0:T(8,128)} %get-tuple-element.72), channel_id=1, source_target_pairs={{1,15},{3,1},{5,3},{7,5},{9,7},{11,9},{13,11},{15,13},{17,31},{19,... | collective-permute-start | bytes 147464 | tf_op jit(solution)/shard_map/ppermute | solution.py:39
  89.7 12.3 %collective-permute-start.3 = (f32[32,128]{1,0:T(8,128)S(1)}, f32[32,128]{1,0:T(8,128)S(1)}, u32[]{:S(2)}, u32[]{:S(2)}) collective-permute-start(f32[32,128]{1,0:T(8,128)S(1)} %slice_select_fusion.3), channel_id=1, source_target_pairs={{0,1},{1,0},{2,3},{3,2},{4,5},{5,4},{6,7},{7,6},{8,9},{9,8},{10,11... | collective-permute-start | bytes 49160 | tf_op jit(solution)/shard_map/ppermute | solution.py:39
  102.1 0.8 collective-permute-done.3
  102.9 5.6 %collective-permute-done.4 = f32[96,128]{1,0:T(8,128)S(1)} collective-permute-done((f32[96,128]{1,0:T(8,128)}, f32[96,128]{1,0:T(8,128)S(1)}, u32[]{:S(2)}, u32[]{:S(2)}) %collective-permute-start.4) | collective-permute-done | bytes 49184 | tf_op jit(solution)/shard_map/ppermute | solution.py:39
  108.5 0.6 pad_maximum_fusion.1
  (9 shorter events, 0.1 us)
Async XLA Ops:
  0.0 18.9 %collective-permute-start = (bf16[4,500,512]{2,0,1:T(4,128)(2,1)}, bf16[4,500,512]{2,0,1:T(4,128)(2,1)S(1)}, u32[]{:S(2)}, u32[]{:S(2)}) collective-permute-start(bf16[4,500,512]{2,0,1:T(4,128)(2,1)} %param.7), channel_id=1, source_target_pairs={{0,1},{1,0},{2,3},{3,2},{4,5},{5,4},{6,7},{7,6},{8,9},{9,8},{10,11... | collective-permute-start | bytes 6144008 | tf_op jit(solution)/shard_map/ppermute | solution.py:39
  2.6 41.3 %collective-permute-start.1 = (bf16[4,500,512]{2,0,1:T(4,128)(2,1)}, bf16[4,500,512]{2,0,1:T(4,128)(2,1)}, u32[]{:S(2)}, u32[]{:S(2)}) collective-permute-start(bf16[4,500,512]{2,0,1:T(4,128)(2,1)} %param.7), channel_id=1, source_target_pairs={{1,3},{2,0},{3,5},{4,2},{5,7},{6,4},{9,11},{10,8},{11,13},{12,10},... | collective-permute-start | bytes 6144008 | tf_op jit(solution)/shard_map/ppermute | solution.py:39
  3.9 64.6 %collective-permute-start.2 = (bf16[4,500,512]{2,0,1:T(4,128)(2,1)}, bf16[4,500,512]{2,0,1:T(4,128)(2,1)}, u32[]{:S(2)}, u32[]{:S(2)}) collective-permute-start(bf16[4,500,512]{2,0,1:T(4,128)(2,1)} %param.7), channel_id=1, source_target_pairs={{0,14},{7,9},{8,6},{15,1},{16,30},{23,25},{24,22},{31,17},{32,46},... | collective-permute-start | bytes 6144008 | tf_op jit(solution)/shard_map/ppermute | solution.py:39
  82.6 25.8 %collective-permute-start.4 = (f32[96,128]{1,0:T(8,128)}, f32[96,128]{1,0:T(8,128)S(1)}, u32[]{:S(2)}, u32[]{:S(2)}) collective-permute-start(f32[96,128]{1,0:T(8,128)} %get-tuple-element.72), channel_id=1, source_target_pairs={{1,15},{3,1},{5,3},{7,5},{9,7},{11,9},{13,11},{15,13},{17,31},{19,... | collective-permute-start | bytes 147464 | tf_op jit(solution)/shard_map/ppermute | solution.py:39
  89.7 13.2 %collective-permute-start.3 = (f32[32,128]{1,0:T(8,128)S(1)}, f32[32,128]{1,0:T(8,128)S(1)}, u32[]{:S(2)}, u32[]{:S(2)}) collective-permute-start(f32[32,128]{1,0:T(8,128)S(1)} %slice_select_fusion.3), channel_id=1, source_target_pairs={{0,1},{1,0},{2,3},{3,2},{4,5},{5,4},{6,7},{7,6},{8,9},{9,8},{10,11... | collective-permute-start | bytes 49160 | tf_op jit(solution)/shard_map/ppermute | solution.py:39

commit v3 on v1

v3 whole, which is shorter than its diff:
```python
import functools

import jax
import jax.numpy as jnp
from jax import lax
from jax.experimental import pallas as pl
from jax.experimental.pallas import tpu as pltpu
from jax.sharding import Mesh, PartitionSpec as P

SIZES = {"zl": 4, "y": 8, "zh": 2, "x": 4, "c": 2}
AUX = ("zl", "y")
BASIS = ("zh", "x", "c")


def send(value, axes, target):
    sizes = [SIZES[a] for a in axes]
    count = 1
    for size in sizes:
        count *= size

    def coords(index):
        out = []
        for size in reversed(sizes):
            out.append(index % size)
            index //= size
        return tuple(reversed(out))

    def flat(position):
        index = 0
        for size, p in zip(sizes, position):
            index = index * size + p
        return index

    pairs = []
    for i in range(count):
        to = target(*coords(i))
        if to is not None:
            pairs.append((i, flat(to)))
    return lax.ppermute(value, axes, pairs)


def along_x(zh, x, c):
    if c == 0:
        return (zh, x - 1, 0) if x > 0 else None
    return (zh, x + 1, 1) if x < 3 else None


def across_z(zh, x, c):
    if c == 0 and x == 0:
        return (1 - zh, 3, 0)
    if c == 1 and x == 3:
        return (1 - zh, 0, 1)
    return None


def to_previous_chip(zh, x, c):
    if c == 0:
        return None
    return (zh, x - 1, 1) if x > 0 else (1 - zh, 3, 1)


def other_core(c):
    return (1 - c,)


def product(a, b):
    return lax.dot_general(a, b, (((0,), (0,)), ((), ())), preferred_element_type=jnp.float32)


def columns(ref, low=0, high=512):
    return ref[:, :, low:high].reshape(-1, high - low)


def put(out, tile, place, base, cols, row_low=0, col_low=0):
    top = jnp.zeros((8, 128), jnp.float32)
    for low in range(0, tile.shape[0], 8):
        owner, r = (row_low + low) // 16, (row_low + low) // 8 % 2
        for at_col in range(0, tile.shape[1], 128):
            piece = tile[low : low + 8, at_col : at_col + 128]
            row = base + (r * cols + col_low + at_col) // 128 * 8
            lead, at = place(owner, row)
            if place(owner, row + 4) == (lead, at + 4):
                out[lead, at : at + 8, :] = piece
            else:
                out[lead, at : at + 4, :] = piece[:4]
                lead, at = place(owner, row + 4)
                out[lead, at : at + 4, :] = piece[4:]
            top = jnp.maximum(top, jnp.abs(piece))
    return top


def power_of(top):
    top = jnp.max(top, axis=(0, 1), keepdims=True)
    return jnp.clip(jnp.floor(jnp.log2(jnp.maximum(top, 1e-30))), -100.0, 100.0)


def by_slice(owner, row):
    if row < 64:
        return row // 8, owner * 12 + row % 8
    return (row - 64) // 4, owner * 12 + 8 + row % 4


def by_owner(owner, row):
    return owner % 8, owner // 8 * 192 + row


def by_device(owner, row):
    return owner, row


def early_half(core, own, beside):
    if core == 0:
        return product(columns(own), columns(beside, 0, 256))
    return product(columns(beside), columns(own, 256, 512))


def finish(out, rows, top):
    power = power_of(top)
    out[:, :rows, :] = out[:, :rows, :] * jnp.exp2(13.0 - power)[None]
    return power[None]


def early_kernel(flags, own, beside, out, top):
    def form(core):
        largest = put(out, product(columns(own), columns(own)), by_slice, 0, 512)
        top[...] = jnp.maximum(largest, put(out, early_half(core, own, beside), by_slice, 64, 256))

    for core in (0, 1):
        pl.when(flags[0] == core)(functools.partial(form, core))
    out[:, 384:, :] = jnp.broadcast_to(finish(out, 384, top[...]), (8, 8, 128))


def late_kernel(flags, own, beside, moved, *rest):
    out, top, own_here, beside_here, moved_here, arrived = rest[-6:]
    early = rest[0] if len(rest) == 7 else None
    place, base = (by_owner, 96) if early is None else (by_device, 0)

    def fetch(n, source, target, low, high):
        return pltpu.make_async_copy(source.at[:, :, low:high], target.at[:, :, low:high], arrived.at[n])

    copies = [
        fetch(0, own, own_here, 0, 512),
        fetch(1, moved, moved_here, 0, 256),
        fetch(2, moved, moved_here, 256, 512),
        fetch(3, beside, beside_here, 0, 512),
    ]
    for copy in copies:
        copy.start()

    def form(core):
        copies[0].wait()
        tops = []
        if early is None:
            tops.append(put(out, product(columns(own_here), columns(own_here)), place, 0, 512))
        for n, low in ((1, 0), (2, 256)):
            copies[n].wait()
            part = columns(moved_here, low, low + 256)
            if core == 0:
                tops.append(put(out, product(columns(own_here), part), place, base, 512, col_low=low))
            else:
                tops.append(put(out, product(part, columns(own_here)), place, base, 512, row_low=low))
        copies[3].wait()
        if core == 0:
            half = product(columns(beside_here), columns(moved_here, 0, 256))
        else:
            half = product(columns(moved_here), columns(beside_here, 256, 512))
        tops.append(put(out, half, place, base + 64, 256))
        if early is None:
            tops.append(put(out, early_half(core, own_here, beside_here), place, 64, 256))
        top[...] = functools.reduce(jnp.maximum, tops)

    for core in (0, 1):
        pl.when(flags[0] == core)(functools.partial(form, core))
    if early is None:
        out[:, 768:, :] = jnp.broadcast_to(finish(out, 768, top[...]), (8, 8, 128))
        return
    out[:, 108:110, :] = jnp.broadcast_to(finish(out, 96, top[...]), (32, 2, 128))
    sums = early[...]
    power = power_of(jnp.max(jnp.abs(sums), axis=0))
    out[:, 96:108, :] = sums * jnp.exp2(13.0 - power)[None]
    out[:, 110:, :] = jnp.broadcast_to(power[None], (32, 2, 128))


def call(kernel, shape, flags, blocks, early=()):
    vmem = pl.BlockSpec(memory_space=pltpu.VMEM)
    blocks = [block.transpose(1, 0, 2) for block in blocks]
    specs = [vmem] * len(blocks)
    scratch = [pltpu.VMEM((8, 128), jnp.float32)]
    if kernel is late_kernel:
        specs = [pl.BlockSpec(memory_space=pl.ANY)] * len(blocks) + [vmem] * len(early)
        scratch += [pltpu.VMEM(blocks[0].shape, jnp.bfloat16)] * 3 + [pltpu.SemaphoreType.DMA((4,))]
    return pl.pallas_call(
        kernel,
        out_shape=jax.ShapeDtypeStruct(shape, jnp.float32),
        in_specs=[pl.BlockSpec(memory_space=pltpu.SMEM)] + specs,
        out_specs=vmem,
        scratch_shapes=scratch,
        compiler_params=pltpu.CompilerParams(vmem_limit_bytes=40 << 20),
        cost_estimate=pl.CostEstimate(flops=1_600_000_000, bytes_accessed=8_000_000, transcendentals=0),
    )(flags, *blocks, *early).astype(jnp.float16)


def untiled(value, cols):
    return value.reshape(2, cols // 128, 8, 128).transpose(0, 2, 1, 3).reshape(16, cols)


def unscaled(parts, power):
    return parts.astype(jnp.float32) * jnp.exp2(power.astype(jnp.float32) - 13.0)[:, None, None]


def on_device(own):
    core = lax.axis_index("c")
    x = lax.axis_index("x")
    first = core == 0
    at_end = jnp.where(first, x == 3, x == 0)
    flags = jnp.stack([core, core])

    kind = jnp.where(at_end, 2, jnp.where((x == 0) | (x == 3), 1, 0))

    along = send(own, BASIS, along_x)
    crossed = send(own, BASIS, across_z)

    def zeros(*shapes):
        return tuple(jnp.zeros(shape + (128,), jnp.float32) for shape in shapes)

    def sum_over_y(parts):
        parts = lax.all_to_all(parts, "y", 0, 0, tiled=True)
        return jnp.sum(unscaled(parts[:, :-8], parts[:, -1, 0]), axis=0)

    def form_early():
        beside = send(own, ("c",), other_core)
        (sums,) = lax.cond(
            kind == 1,
            lambda: zeros((384,)),
            lambda: (sum_over_y(call(early_kernel, (8, 392, 128), flags, (own, beside))),),
        )
        return sums.reshape(32, 12, 128), beside

    def late_over_aux(moved):
        parts = call(late_kernel, (32, 112, 128), flags, (own, beside, moved), (early_sums,))
        parts = lax.all_to_all(parts, AUX, 0, 0, tiled=True)
        late = jnp.sum(unscaled(parts[:, :96], parts[:, 108, 0]), axis=0)
        early = jnp.sum(unscaled(parts[:, 96:108], parts[:, 110, 0]).reshape(4, 8, 12, 128), axis=0)
        return jnp.concatenate([early[:, :8].reshape(64, 128), early[:, 8:].reshape(32, 128), late])

    def all_over_y():
        return sum_over_y(call(late_kernel, (8, 776, 128), flags, (own, beside, along)))

    def over_z():
        return jnp.sum(lax.all_to_all(sums_y.reshape(4, 192, 128), "zl", 0, 0, tiled=True), axis=0)

    early_sums, beside = lax.cond(core < 2, form_early, lambda: zeros((32, 12)) + (own,))
    early_sums, along = lax.optimization_barrier((early_sums, along))
    sums, sums_y = lax.switch(
        kind,
        [
            lambda: (late_over_aux(along),) + zeros((768,)),
            lambda: zeros((192,)) + (all_over_y(),),
            lambda: zeros((192,), (768,)),
        ],
    )
    sums, sums_y, crossed = lax.optimization_barrier((sums, sums_y, crossed))
    sums = lax.switch(kind, [lambda: sums, over_z, lambda: late_over_aux(crossed)])
    early, late = sums[:96], sums[96:]

    swapped = send(jnp.where(first, late[64:], early[64:]), ("c",), other_core)
    back = send(late, BASIS, to_previous_chip)

    s0 = untiled(early[:64], 512)
    left = untiled(jnp.where(first, early[64:], swapped), 256)
    right = untiled(jnp.where(first, swapped, back[64:]), 256)
    s1 = jnp.concatenate([left, right], axis=1)
    s2 = untiled(jnp.where(first, late[:64], back[:64]), 512)
    return jnp.stack([s0, s1, s2])


def solution(mesh):
    fine = Mesh(mesh.devices.reshape(tuple(SIZES.values())), tuple(SIZES))
    return jax.shard_map(
        on_device, mesh=fine, in_specs=(P(AUX, None, BASIS),), out_specs=P(None, BASIS + AUX, None), check_vma=False
    )
```

time: 124 us -> 102 us (0.82)
  the two profiles are of different devices: /device:TPU:9 before, /device:TPU:15 now
where the time goes in v3:
time: 102 us
  blocking collectives  43.2 us (42%)
  starting transfers between devices  35 us (34%)
  waiting for transfers between devices  13.7 us (13%)
  Pallas kernels  6.87 us (7%)
  other arithmetic  1.53 us (2%)
    ppermute x5, starting transfers between devices, send(): return lax.ppermute(value, axes, pairs)  35 us
    all_to_all x1, blocking collectives, sum_over_y(): parts = lax.all_to_all(parts, 'y', 0, 0, tiled=True)  30.6 us
    ppermute x5, waiting for transfers between devices, send(): return lax.ppermute(value, axes, pairs)  13.7 us
    all_to_all x1, blocking collectives, over_z(): lax.all_to_all(sums_y.reshape(4, 192, 128), 'zl', 0, 0, tiled=True)  12.6 us
    pallas_call x1, Pallas kernels, call(): pl.pallas_call(kernel, out_shape=jax.ShapeDtypeStruct(shape, jnp.float32)...  6.87 us
  transfers between devices with their start and end apart: 5, of which 4 were waited for; matrix products, arithmetic and copies ran while one was open for 2% of the time, Pallas kernels for 7%

profile of v3, /device:TPU:15, one launch (start us, length us, event | category | flops | bytes accessed | tf_op | source)
XLA Modules:
  0.0 101.7 jit_solution(3603335832792355965)
XLA Ops:
  0.0 1.3 %collective-permute-start.1 = (bf16[4,500,512]{2,0,1:T(4,128)(2,1)}, bf16[4,500,512]{2,0,1:T(4,128)(2,1)S(1)}, u32[]{:S(2)}, u32[]{:S(2)}) collective-permute-start(bf16[4,500,512]{2,0,1:T(4,128)(2,1)} %param.11), channel_id=1, source_target_pairs={{1,3},{2,0},{3,5},{4,2},{5,7},{6,4},{9,11},{10,8},{11,13},{12,10},... | collective-permute-start | bytes 6144008 | tf_op jit(solution)/shard_map/ppermute | solution.py:39
  1.3 13.8 %collective-permute-start.2 = (bf16[4,500,512]{2,0,1:T(4,128)(2,1)}, bf16[4,500,512]{2,0,1:T(4,128)(2,1)}, u32[]{:S(2)}, u32[]{:S(2)}) collective-permute-start(bf16[4,500,512]{2,0,1:T(4,128)(2,1)} %param.11), channel_id=1, source_target_pairs={{0,14},{7,9},{8,6},{15,1},{16,30},{23,25},{24,22},{31,17},{32,46},... | collective-permute-start | bytes 6144008 | tf_op jit(solution)/shard_map/ppermute | solution.py:39
  15.1 0.1 pad_add_fusion
  15.2 7.0 %conditional.4 = (f32[32,12,128]{2,1,0:T(8,128)}, bf16[4,500,512]{2,0,1:T(4,128)(2,1)}) conditional(s32[]{:T(128)} %convert_element_type.60, bf16[4,500,512]{2,0,1:T(4,128)(2,1)} %param.11, (s32[]{:T(128)}, bf16[4,500,512]{2,0,1:T(4,128)(2,1)}, s32[2]{0:T(128)S(1)}) %tuple.44), branch_computations={%region_0.1_spmd, %region_1.5_spmd} | conditional | flops 1601531904 | bytes 21582518 | solution.py:252
  15.2 1.9 %collective-permute-start = (bf16[4,500,512]{2,0,1:T(4,128)(2,1)}, bf16[4,500,512]{2,0,1:T(4,128)(2,1)}, u32[]{:S(2)}, u32[]{:S(2)}) collective-permute-start(bf16[4,500,512]{2,0,1:T(4,128)(2,1)} %get-tuple-element.60), channel_id=1, source_target_pairs={{0,1},{1,0},{2,3},{3,2},{4,5},{5,4},{6,7},{7,6},{8,9},{9,8},{10,11... | collective-permute-start | bytes 6144008 | tf_op jit(solution)/shard_map/cond/branch_1_fun/ppermute | solution.py:39
  17.1 4.4 %collective-permute-done = bf16[4,500,512]{2,0,1:T(4,128)(2,1)} collective-permute-done((bf16[4,500,512]{2,0,1:T(4,128)(2,1)}, bf16[4,500,512]{2,0,1:T(4,128)(2,1)}, u32[]{:S(2)}, u32[]{:S(2)}) %collective-permute-start) | collective-permute-done | bytes 2048032 | tf_op jit(solution)/shard_map/cond/branch_1_fun/ppermute | solution.py:39
  21.5 0.7 conditional
  21.5 0.7 reshape.32
  22.2 4.6 %collective-permute-done.1 = bf16[4,500,512]{2,0,1:T(4,128)(2,1)S(1)} collective-permute-done((bf16[4,500,512]{2,0,1:T(4,128)(2,1)}, bf16[4,500,512]{2,0,1:T(4,128)(2,1)S(1)}, u32[]{:S(2)}, u32[]{:S(2)}) %collective-permute-start.1) | collective-permute-done | bytes 2048032 | tf_op jit(solution)/shard_map/ppermute | solution.py:39
  26.9 38.8 %conditional.5 = (f32[192,128]{1,0:T(8,128)S(1)}, f32[768,128]{1,0:T(8,128)S(1)}) conditional(s32[]{:T(128)} %clamp.4, (bf16[4,500,512]{2,0,1:T(4,128)(2,1)}, bf16[4,500,512]{2,0,1:T(4,128)(2,1)}, bf16[4,500,512]{2,0,1:T(4,128)(2,1)S(1)}, s32[2]{0:T(128)S(1)}, f32[32,12,128]{2,1,0:T(8,128)}) %tuple.46, ...), branch_computations={%region_5.8_spmd, %region_8.10_spmd, %region_10.11_spmd} | conditional | flops 1603055616 | bytes 18010724 | solution.py:254
  26.9 6.9 %branch_1_fun.1 = f32[8,776,128]{2,1,0:T(8,128)S(1)} custom-call(s32[2]{0:T(128)S(1)} %get-tuple-element.67.flags, bf16[500,4,512]{2,1,0:T(4,128)(2,1)} %bitcast.45, bf16[500,4,512]{2,1,0:T(4,128)(2,1)} %bitcast.9.beside, bf16[500,4,512]{2,1,0:T(4,128)(2,1)S(1)} %bitcast.48), custom_call_target="tpu_custom_call" | custom-call | flops 1600000000 | bytes 8000000 | tf_op jit(solution)/shard_map/cond/branch_1_fun/pallas_call | solution.py:192
  33.7 0.2 convert_element_type.51
  34.0 30.6 %all_to_all.22 = f16[8,776,128]{2,1,0:T(8,128)(2,1)S(1)} all-to-all(f16[8,776,128]{2,1,0:T(8,128)(2,1)S(1)} %convert_element_type.51), channel_id=1, replica_groups=mesh['zl'=4,'y'=8,'zh'=2,'x'=4,'c'=2] {'y'}, dimensions={0} | all-to-all | bytes 3178496 | tf_op jit(solution)/shard_map/cond/branch_1_fun/all_to_all | solution.py:227
  64.6 0.2 fusion.15
  64.8 0.4 multiply_reduce_fusion.2
  65.7 0.0 collective-permute-done.2
  65.7 12.6 %conditional.6 = (f32[192,128]{1,0:T(8,128)S(1)}) conditional(s32[]{:T(128)} %clamp.4, f32[192,128]{1,0:T(8,128)S(1)} %get-tuple-element.91, f32[768,128]{1,0:T(8,128)S(1)} %get-tuple-element.92, (bf16[4,500,512]{2,0,1:T(4,128)(2,1)}, bf16[4,500,512]{2,0,1:T(4,128)(2,1)}, bf16[4,500,512]{2,0,1:T(4,128)(2,1)}, s32[2]{0:T(128)S(1)}, ...), branch_computations={%region_11.12_spmd, %region_12.14_spmd, %region_14.17_spmd} | conditional | flops 1601810688 | bytes 14259340 | solution.py:263
  65.7 12.6 %all_to_all.23 = f32[4,192,128]{2,1,0:T(8,128)S(1)} all-to-all(f32[4,192,128]{2,1,0:T(8,128)S(1)} %bitcast.49), channel_id=1, replica_groups=mesh['zl'=4,'y'=8,'zh'=2,'x'=4,'c'=2] {'zl'}, dimensions={0} | all-to-all | bytes 786432 | tf_op jit(solution)/shard_map/cond/branch_1_fun/all_to_all | solution.py:250
  78.3 7.3 %collective-permute-start.4 = (f32[96,128]{1,0:T(8,128)S(1)}, f32[96,128]{1,0:T(8,128)S(1)}, u32[]{:S(2)}, u32[]{:S(2)}) collective-permute-start(f32[96,128]{1,0:T(8,128)S(1)} %slice.101), channel_id=1, source_target_pairs={{1,15},{3,1},{5,3},{7,5},{9,7},{11,9},{13,11},{15,13},{17,31},{19,... | collective-permute-start | bytes 147464 | tf_op jit(solution)/shard_map/ppermute | solution.py:39
  85.6 10.7 %collective-permute-start.3 = (f32[32,128]{1,0:T(8,128)S(1)}, f32[32,128]{1,0:T(8,128)S(1)}, u32[]{:S(2)}, u32[]{:S(2)}) collective-permute-start(f32[32,128]{1,0:T(8,128)S(1)} %slice_select_fusion.2), channel_id=1, source_target_pairs={{0,1},{1,0},{2,3},{3,2},{4,5},{5,4},{6,7},{7,6},{8,9},{9,8},{10,11... | collective-permute-start | bytes 49160 | tf_op jit(solution)/shard_map/ppermute | solution.py:39
  96.4 0.8 collective-permute-done.3
  97.2 3.8 %collective-permute-done.4 = f32[96,128]{1,0:T(8,128)S(1)} collective-permute-done((f32[96,128]{1,0:T(8,128)S(1)}, f32[96,128]{1,0:T(8,128)S(1)}, u32[]{:S(2)}, u32[]{:S(2)}) %collective-permute-start.4) | collective-permute-done | bytes 49184 | tf_op jit(solution)/shard_map/ppermute | solution.py:39
  101.0 0.6 pad_maximum_fusion.2
  (7 shorter events, 0.1 us)
Async XLA Ops:
  0.0 26.9 %collective-permute-start.1 = (bf16[4,500,512]{2,0,1:T(4,128)(2,1)}, bf16[4,500,512]{2,0,1:T(4,128)(2,1)S(1)}, u32[]{:S(2)}, u32[]{:S(2)}) collective-permute-start(bf16[4,500,512]{2,0,1:T(4,128)(2,1)} %param.11), channel_id=1, source_target_pairs={{1,3},{2,0},{3,5},{4,2},{5,7},{6,4},{9,11},{10,8},{11,13},{12,10},... | collective-permute-start | bytes 6144008 | tf_op jit(solution)/shard_map/ppermute | solution.py:39
  1.3 64.4 %collective-permute-start.2 = (bf16[4,500,512]{2,0,1:T(4,128)(2,1)}, bf16[4,500,512]{2,0,1:T(4,128)(2,1)}, u32[]{:S(2)}, u32[]{:S(2)}) collective-permute-start(bf16[4,500,512]{2,0,1:T(4,128)(2,1)} %param.11), channel_id=1, source_target_pairs={{0,14},{7,9},{8,6},{15,1},{16,30},{23,25},{24,22},{31,17},{32,46},... | collective-permute-start | bytes 6144008 | tf_op jit(solution)/shard_map/ppermute | solution.py:39
  15.2 6.3 %collective-permute-start = (bf16[4,500,512]{2,0,1:T(4,128)(2,1)}, bf16[4,500,512]{2,0,1:T(4,128)(2,1)}, u32[]{:S(2)}, u32[]{:S(2)}) collective-permute-start(bf16[4,500,512]{2,0,1:T(4,128)(2,1)} %get-tuple-element.60), channel_id=1, source_target_pairs={{0,1},{1,0},{2,3},{3,2},{4,5},{5,4},{6,7},{7,6},{8,9},{9,8},{10,11... | collective-permute-start | bytes 6144008 | tf_op jit(solution)/shard_map/cond/branch_1_fun/ppermute | solution.py:39
  78.3 22.7 %collective-permute-start.4 = (f32[96,128]{1,0:T(8,128)S(1)}, f32[96,128]{1,0:T(8,128)S(1)}, u32[]{:S(2)}, u32[]{:S(2)}) collective-permute-start(f32[96,128]{1,0:T(8,128)S(1)} %slice.101), channel_id=1, source_target_pairs={{1,15},{3,1},{5,3},{7,5},{9,7},{11,9},{13,11},{15,13},{17,31},{19,... | collective-permute-start | bytes 147464 | tf_op jit(solution)/shard_map/ppermute | solution.py:39
  85.6 11.5 %collective-permute-start.3 = (f32[32,128]{1,0:T(8,128)S(1)}, f32[32,128]{1,0:T(8,128)S(1)}, u32[]{:S(2)}, u32[]{:S(2)}) collective-permute-start(f32[32,128]{1,0:T(8,128)S(1)} %slice_select_fusion.2), channel_id=1, source_target_pairs={{0,1},{1,0},{2,3},{3,2},{4,5},{5,4},{6,7},{7,6},{8,9},{9,8},{10,11... | collective-permute-start | bytes 49160 | tf_op jit(solution)/shard_map/ppermute | solution.py:39

commit v4 on v3

--- a/solution.py
+++ b/solution.py
@@ -114,9 +114,14 @@
     return product(columns(beside), columns(own, 256, 512))
 
 
+def coded(value, power):
+    value = value * jnp.exp2(6.0 - power)[None]
+    return value * jnp.abs(value)
+
+
 def finish(out, rows, top):
     power = power_of(top)
-    out[:, :rows, :] = out[:, :rows, :] * jnp.exp2(13.0 - power)[None]
+    out[:, :rows, :] = coded(out[:, :rows, :], power)
     return power[None]
 
 
@@ -177,7 +182,7 @@
     out[:, 108:110, :] = jnp.broadcast_to(finish(out, 96, top[...]), (32, 2, 128))
     sums = early[...]
     power = power_of(jnp.max(jnp.abs(sums), axis=0))
-    out[:, 96:108, :] = sums * jnp.exp2(13.0 - power)[None]
+    out[:, 96:108, :] = coded(sums, power)
     out[:, 110:, :] = jnp.broadcast_to(power[None], (32, 2, 128))
 
 
@@ -204,8 +209,10 @@
     return value.reshape(2, cols // 128, 8, 128).transpose(0, 2, 1, 3).reshape(16, cols)
 
 
-def unscaled(parts, power):
-    return parts.astype(jnp.float32) * jnp.exp2(power.astype(jnp.float32) - 13.0)[:, None, None]
+def decoded(parts, power):
+    parts = parts.astype(jnp.float32)
+    value = parts * lax.rsqrt(jnp.maximum(jnp.abs(parts), 1e-30))
+    return value * jnp.exp2(power.astype(jnp.float32) - 6.0)[:, None, None]
 
 
 def on_device(own):
@@ -225,7 +232,7 @@
 
     def sum_over_y(parts):
         parts = lax.all_to_all(parts, "y", 0, 0, tiled=True)
-        return jnp.sum(unscaled(parts[:, :-8], parts[:, -1, 0]), axis=0)
+        return jnp.sum(decoded(parts[:, :-8], parts[:, -1, 0]), axis=0)
 
     def form_early():
         beside = send(own, ("c",), other_core)
@@ -239,8 +246,8 @@
     def late_over_aux(moved):
         parts = call(late_kernel, (32, 112, 128), flags, (own, beside, moved), (early_sums,))
         parts = lax.all_to_all(parts, AUX, 0, 0, tiled=True)
-        late = jnp.sum(unscaled(parts[:, :96], parts[:, 108, 0]), axis=0)
-        early = jnp.sum(unscaled(parts[:, 96:108], parts[:, 110, 0]).reshape(4, 8, 12, 128), axis=0)
+        late = jnp.sum(decoded(parts[:, :96], parts[:, 108, 0]), axis=0)
+        early = jnp.sum(decoded(parts[:, 96:108], parts[:, 110, 0]).reshape(4, 8, 12, 128), axis=0)
         return jnp.concatenate([early[:, :8].reshape(64, 128), early[:, 8:].reshape(32, 128), late])
 
     def all_over_y():

time: 102 us -> 102 us (level)
  no operation moved by 1% of the time
where the time goes in v4:
time: 102 us
  blocking collectives  43.3 us (42%)
  starting transfers between devices  34.5 us (34%)
  waiting for transfers between devices  13.7 us (13%)
  Pallas kernels  7.16 us (7%)
  other arithmetic  1.96 us (2%)
    ppermute x5, starting transfers between devices, send(): return lax.ppermute(value, axes, pairs)  34.5 us
    all_to_all x1, blocking collectives, sum_over_y(): parts = lax.all_to_all(parts, 'y', 0, 0, tiled=True)  30.5 us
    ppermute x5, waiting for transfers between devices, send(): return lax.ppermute(value, axes, pairs)  13.7 us
    all_to_all x1, blocking collectives, over_z(): lax.all_to_all(sums_y.reshape(4, 192, 128), 'zl', 0, 0, tiled=True)  12.8 us
    pallas_call x1, Pallas kernels, call(): pl.pallas_call(kernel, out_shape=jax.ShapeDtypeStruct(shape, jnp.float32)...  7.16 us
  transfers between devices with their start and end apart: 5, of which 4 were waited for; matrix products, arithmetic and copies ran while one was open for 2% of the time, Pallas kernels for 7%

profile of v4, /device:TPU:15, one launch (start us, length us, event | category | flops | bytes accessed | tf_op | source)
XLA Modules:
  0.0 102.0 jit_solution(1181875978566358684)
XLA Ops:
  0.0 1.3 %collective-permute-start.1 = (bf16[4,500,512]{2,0,1:T(4,128)(2,1)}, bf16[4,500,512]{2,0,1:T(4,128)(2,1)S(1)}, u32[]{:S(2)}, u32[]{:S(2)}) collective-permute-start(bf16[4,500,512]{2,0,1:T(4,128)(2,1)} %param.11), channel_id=1, source_target_pairs={{1,3},{2,0},{3,5},{4,2},{5,7},{6,4},{9,11},{10,8},{11,13},{12,10},... | collective-permute-start | bytes 6144008 | tf_op jit(solution)/shard_map/ppermute | solution.py:39
  1.3 13.8 %collective-permute-start.2 = (bf16[4,500,512]{2,0,1:T(4,128)(2,1)}, bf16[4,500,512]{2,0,1:T(4,128)(2,1)}, u32[]{:S(2)}, u32[]{:S(2)}) collective-permute-start(bf16[4,500,512]{2,0,1:T(4,128)(2,1)} %param.11), channel_id=1, source_target_pairs={{0,14},{7,9},{8,6},{15,1},{16,30},{23,25},{24,22},{31,17},{32,46},... | collective-permute-start | bytes 6144008 | tf_op jit(solution)/shard_map/ppermute | solution.py:39
  15.1 0.1 pad_add_fusion
  15.2 7.0 %conditional.4 = (f32[32,12,128]{2,1,0:T(8,128)}, bf16[4,500,512]{2,0,1:T(4,128)(2,1)}) conditional(s32[]{:T(128)} %convert_element_type.60, bf16[4,500,512]{2,0,1:T(4,128)(2,1)} %param.11, (s32[]{:T(128)}, bf16[4,500,512]{2,0,1:T(4,128)(2,1)}, s32[2]{0:T(128)S(1)}) %tuple.44), branch_computations={%region_0.1_spmd, %region_1.5_spmd} | conditional | flops 1602711552 | bytes 21582518 | solution.py:259
  15.2 1.9 %collective-permute-start = (bf16[4,500,512]{2,0,1:T(4,128)(2,1)}, bf16[4,500,512]{2,0,1:T(4,128)(2,1)}, u32[]{:S(2)}, u32[]{:S(2)}) collective-permute-start(bf16[4,500,512]{2,0,1:T(4,128)(2,1)} %get-tuple-element.60), channel_id=1, source_target_pairs={{0,1},{1,0},{2,3},{3,2},{4,5},{5,4},{6,7},{7,6},{8,9},{9,8},{10,11... | collective-permute-start | bytes 6144008 | tf_op jit(solution)/shard_map/cond/branch_1_fun/ppermute | solution.py:39
  17.1 4.4 %collective-permute-done = bf16[4,500,512]{2,0,1:T(4,128)(2,1)} collective-permute-done((bf16[4,500,512]{2,0,1:T(4,128)(2,1)}, bf16[4,500,512]{2,0,1:T(4,128)(2,1)}, u32[]{:S(2)}, u32[]{:S(2)}) %collective-permute-start) | collective-permute-done | bytes 2048032 | tf_op jit(solution)/shard_map/cond/branch_1_fun/ppermute | solution.py:39
  21.5 0.7 conditional
  21.5 0.7 reshape.32
  22.2 4.6 %collective-permute-done.1 = bf16[4,500,512]{2,0,1:T(4,128)(2,1)S(1)} collective-permute-done((bf16[4,500,512]{2,0,1:T(4,128)(2,1)}, bf16[4,500,512]{2,0,1:T(4,128)(2,1)S(1)}, u32[]{:S(2)}, u32[]{:S(2)}) %collective-permute-start.1) | collective-permute-done | bytes 2048032 | tf_op jit(solution)/shard_map/ppermute | solution.py:39
  26.9 39.4 %conditional.5 = (f32[192,128]{1,0:T(8,128)S(1)}, f32[768,128]{1,0:T(8,128)S(1)}) conditional(s32[]{:T(128)} %clamp.4, (bf16[4,500,512]{2,0,1:T(4,128)(2,1)}, bf16[4,500,512]{2,0,1:T(4,128)(2,1)}, bf16[4,500,512]{2,0,1:T(4,128)(2,1)S(1)}, s32[2]{0:T(128)S(1)}, f32[32,12,128]{2,1,0:T(8,128)}) %tuple.46, ...), branch_computations={%region_5.8_spmd, %region_8.10_spmd, %region_10.11_spmd} | conditional | flops 1605414912 | bytes 18010724 | solution.py:261
  26.9 7.2 %branch_1_fun.1 = f32[8,776,128]{2,1,0:T(8,128)S(1)} custom-call(s32[2]{0:T(128)S(1)} %get-tuple-element.67.flags, bf16[500,4,512]{2,1,0:T(4,128)(2,1)} %bitcast.45, bf16[500,4,512]{2,1,0:T(4,128)(2,1)} %bitcast.9.beside, bf16[500,4,512]{2,1,0:T(4,128)(2,1)S(1)} %bitcast.48), custom_call_target="tpu_custom_call" | custom-call | flops 1600000000 | bytes 8000000 | tf_op jit(solution)/shard_map/cond/branch_1_fun/pallas_call | solution.py:197
  34.0 0.2 convert_element_type.51
  34.2 30.5 %all_to_all.22 = f16[8,776,128]{2,1,0:T(8,128)(2,1)S(1)} all-to-all(f16[8,776,128]{2,1,0:T(8,128)(2,1)S(1)} %convert_element_type.51), channel_id=1, replica_groups=mesh['zl'=4,'y'=8,'zh'=2,'x'=4,'c'=2] {'y'}, dimensions={0} | all-to-all | bytes 3178496 | tf_op jit(solution)/shard_map/cond/branch_1_fun/all_to_all | solution.py:234
  64.7 0.2 fusion.30
  64.9 0.8 fusion.26
  66.2 0.0 collective-permute-done.2
  66.2 12.9 %conditional.6 = (f32[192,128]{1,0:T(8,128)S(1)}) conditional(s32[]{:T(128)} %clamp.4, f32[192,128]{1,0:T(8,128)S(1)} %get-tuple-element.91, f32[768,128]{1,0:T(8,128)S(1)} %get-tuple-element.92, (bf16[4,500,512]{2,0,1:T(4,128)(2,1)}, bf16[4,500,512]{2,0,1:T(4,128)(2,1)}, bf16[4,500,512]{2,0,1:T(4,128)(2,1)}, s32[2]{0:T(128)S(1)}, ...), branch_computations={%region_11.12_spmd, %region_12.14_spmd, %region_14.17_spmd} | conditional | flops 1603137792 | bytes 14259340 | solution.py:270
  66.3 12.8 %all_to_all.23 = f32[4,192,128]{2,1,0:T(8,128)S(1)} all-to-all(f32[4,192,128]{2,1,0:T(8,128)S(1)} %bitcast.49), channel_id=1, replica_groups=mesh['zl'=4,'y'=8,'zh'=2,'x'=4,'c'=2] {'zl'}, dimensions={0} | all-to-all | bytes 786432 | tf_op jit(solution)/shard_map/cond/branch_1_fun/all_to_all | solution.py:257
  79.1 7.1 %collective-permute-start.4 = (f32[96,128]{1,0:T(8,128)S(1)}, f32[96,128]{1,0:T(8,128)S(1)}, u32[]{:S(2)}, u32[]{:S(2)}) collective-permute-start(f32[96,128]{1,0:T(8,128)S(1)} %slice.101), channel_id=1, source_target_pairs={{1,15},{3,1},{5,3},{7,5},{9,7},{11,9},{13,11},{15,13},{17,31},{19,... | collective-permute-start | bytes 147464 | tf_op jit(solution)/shard_map/ppermute | solution.py:39
  86.3 10.4 %collective-permute-start.3 = (f32[32,128]{1,0:T(8,128)S(1)}, f32[32,128]{1,0:T(8,128)S(1)}, u32[]{:S(2)}, u32[]{:S(2)}) collective-permute-start(f32[32,128]{1,0:T(8,128)S(1)} %slice_select_fusion.2), channel_id=1, source_target_pairs={{0,1},{1,0},{2,3},{3,2},{4,5},{5,4},{6,7},{7,6},{8,9},{9,8},{10,11... | collective-permute-start | bytes 49160 | tf_op jit(solution)/shard_map/ppermute | solution.py:39
  96.7 0.8 collective-permute-done.3
  97.5 3.8 %collective-permute-done.4 = f32[96,128]{1,0:T(8,128)S(1)} collective-permute-done((f32[96,128]{1,0:T(8,128)S(1)}, f32[96,128]{1,0:T(8,128)S(1)}, u32[]{:S(2)}, u32[]{:S(2)}) %collective-permute-start.4) | collective-permute-done | bytes 49184 | tf_op jit(solution)/shard_map/ppermute | solution.py:39
  101.4 0.6 pad_maximum_fusion.2
  (7 shorter events, 0.1 us)
Async XLA Ops:
  0.0 26.9 %collective-permute-start.1 = (bf16[4,500,512]{2,0,1:T(4,128)(2,1)}, bf16[4,500,512]{2,0,1:T(4,128)(2,1)S(1)}, u32[]{:S(2)}, u32[]{:S(2)}) collective-permute-start(bf16[4,500,512]{2,0,1:T(4,128)(2,1)} %param.11), channel_id=1, source_target_pairs={{1,3},{2,0},{3,5},{4,2},{5,7},{6,4},{9,11},{10,8},{11,13},{12,10},... | collective-permute-start | bytes 6144008 | tf_op jit(solution)/shard_map/ppermute | solution.py:39
  1.3 64.9 %collective-permute-start.2 = (bf16[4,500,512]{2,0,1:T(4,128)(2,1)}, bf16[4,500,512]{2,0,1:T(4,128)(2,1)}, u32[]{:S(2)}, u32[]{:S(2)}) collective-permute-start(bf16[4,500,512]{2,0,1:T(4,128)(2,1)} %param.11), channel_id=1, source_target_pairs={{0,14},{7,9},{8,6},{15,1},{16,30},{23,25},{24,22},{31,17},{32,46},... | collective-permute-start | bytes 6144008 | tf_op jit(solution)/shard_map/ppermute | solution.py:39
  15.2 6.3 %collective-permute-start = (bf16[4,500,512]{2,0,1:T(4,128)(2,1)}, bf16[4,500,512]{2,0,1:T(4,128)(2,1)}, u32[]{:S(2)}, u32[]{:S(2)}) collective-permute-start(bf16[4,500,512]{2,0,1:T(4,128)(2,1)} %get-tuple-element.60), channel_id=1, source_target_pairs={{0,1},{1,0},{2,3},{3,2},{4,5},{5,4},{6,7},{7,6},{8,9},{9,8},{10,11... | collective-permute-start | bytes 6144008 | tf_op jit(solution)/shard_map/cond/branch_1_fun/ppermute | solution.py:39
  79.1 22.2 %collective-permute-start.4 = (f32[96,128]{1,0:T(8,128)S(1)}, f32[96,128]{1,0:T(8,128)S(1)}, u32[]{:S(2)}, u32[]{:S(2)}) collective-permute-start(f32[96,128]{1,0:T(8,128)S(1)} %slice.101), channel_id=1, source_target_pairs={{1,15},{3,1},{5,3},{7,5},{9,7},{11,9},{13,11},{15,13},{17,31},{19,... | collective-permute-start | bytes 147464 | tf_op jit(solution)/shard_map/ppermute | solution.py:39
  86.3 11.2 %collective-permute-start.3 = (f32[32,128]{1,0:T(8,128)S(1)}, f32[32,128]{1,0:T(8,128)S(1)}, u32[]{:S(2)}, u32[]{:S(2)}) collective-permute-start(f32[32,128]{1,0:T(8,128)S(1)} %slice_select_fusion.2), channel_id=1, source_target_pairs={{0,1},{1,0},{2,3},{3,2},{4,5},{5,4},{6,7},{7,6},{8,9},{9,8},{10,11... | collective-permute-start | bytes 49160 | tf_op jit(solution)/shard_map/ppermute | solution.py:39

commit v5 on v4

--- a/solution.py
+++ b/solution.py
@@ -72,7 +72,7 @@
 
 
 def put(out, tile, place, base, cols, row_low=0, col_low=0):
-    top = jnp.zeros((8, 128), jnp.float32)
+    tops = [jnp.zeros((8, 128), jnp.float32)] * 4
     for low in range(0, tile.shape[0], 8):
         owner, r = (row_low + low) // 16, (row_low + low) // 8 % 2
         for at_col in range(0, tile.shape[1], 128):
@@ -85,8 +85,8 @@
                 out[lead, at : at + 4, :] = piece[:4]
                 lead, at = place(owner, row + 4)
                 out[lead, at : at + 4, :] = piece[4:]
-            top = jnp.maximum(top, jnp.abs(piece))
-    return top
+            tops = tops[1:] + [jnp.maximum(tops[0], jnp.abs(piece))]
+    return functools.reduce(jnp.maximum, tops)
 
 
 def power_of(top):

time: 102 us -> 102 us (level)
  no operation moved by 1% of the time
where the time goes in v5:
time: 102 us
  blocking collectives  43.2 us (42%)
  starting transfers between devices  34.9 us (34%)
  waiting for transfers between devices  13.5 us (13%)
  Pallas kernels  6.9 us (7%)
  other arithmetic  1.96 us (2%)
    ppermute x5, starting transfers between devices, send(): return lax.ppermute(value, axes, pairs)  34.9 us
    all_to_all x1, blocking collectives, sum_over_y(): parts = lax.all_to_all(parts, 'y', 0, 0, tiled=True)  30.7 us
    ppermute x5, waiting for transfers between devices, send(): return lax.ppermute(value, axes, pairs)  13.5 us
    all_to_all x1, blocking collectives, over_z(): lax.all_to_all(sums_y.reshape(4, 192, 128), 'zl', 0, 0, tiled=True)  12.5 us
    pallas_call x1, Pallas kernels, call(): pl.pallas_call(kernel, out_shape=jax.ShapeDtypeStruct(shape, jnp.float32)...  6.9 us
  transfers between devices with their start and end apart: 5, of which 4 were waited for; matrix products, arithmetic and copies ran while one was open for 2% of the time, Pallas kernels for 7%

profile of v5, /device:TPU:15, one launch (start us, length us, event | category | flops | bytes accessed | tf_op | source)
XLA Modules:
  0.0 101.9 jit_solution(4557568690527077495)
XLA Ops:
  0.0 1.3 %collective-permute-start.1 = (bf16[4,500,512]{2,0,1:T(4,128)(2,1)}, bf16[4,500,512]{2,0,1:T(4,128)(2,1)S(1)}, u32[]{:S(2)}, u32[]{:S(2)}) collective-permute-start(bf16[4,500,512]{2,0,1:T(4,128)(2,1)} %param.11), channel_id=1, source_target_pairs={{1,3},{2,0},{3,5},{4,2},{5,7},{6,4},{9,11},{10,8},{11,13},{12,10},... | collective-permute-start | bytes 6144008 | tf_op jit(solution)/shard_map/ppermute | solution.py:39
  1.3 13.8 %collective-permute-start.2 = (bf16[4,500,512]{2,0,1:T(4,128)(2,1)}, bf16[4,500,512]{2,0,1:T(4,128)(2,1)}, u32[]{:S(2)}, u32[]{:S(2)}) collective-permute-start(bf16[4,500,512]{2,0,1:T(4,128)(2,1)} %param.11), channel_id=1, source_target_pairs={{0,14},{7,9},{8,6},{15,1},{16,30},{23,25},{24,22},{31,17},{32,46},... | collective-permute-start | bytes 6144008 | tf_op jit(solution)/shard_map/ppermute | solution.py:39
  15.1 0.1 pad_add_fusion
  15.2 7.0 %conditional.4 = (f32[32,12,128]{2,1,0:T(8,128)}, bf16[4,500,512]{2,0,1:T(4,128)(2,1)}) conditional(s32[]{:T(128)} %convert_element_type.60, bf16[4,500,512]{2,0,1:T(4,128)(2,1)} %param.11, (s32[]{:T(128)}, bf16[4,500,512]{2,0,1:T(4,128)(2,1)}, s32[2]{0:T(128)S(1)}) %tuple.44), branch_computations={%region_0.1_spmd, %region_1.5_spmd} | conditional | flops 1602711552 | bytes 21582518 | solution.py:259
  15.2 1.9 %collective-permute-start = (bf16[4,500,512]{2,0,1:T(4,128)(2,1)}, bf16[4,500,512]{2,0,1:T(4,128)(2,1)}, u32[]{:S(2)}, u32[]{:S(2)}) collective-permute-start(bf16[4,500,512]{2,0,1:T(4,128)(2,1)} %get-tuple-element.60), channel_id=1, source_target_pairs={{0,1},{1,0},{2,3},{3,2},{4,5},{5,4},{6,7},{7,6},{8,9},{9,8},{10,11... | collective-permute-start | bytes 6144008 | tf_op jit(solution)/shard_map/cond/branch_1_fun/ppermute | solution.py:39
  17.1 4.4 %collective-permute-done = bf16[4,500,512]{2,0,1:T(4,128)(2,1)} collective-permute-done((bf16[4,500,512]{2,0,1:T(4,128)(2,1)}, bf16[4,500,512]{2,0,1:T(4,128)(2,1)}, u32[]{:S(2)}, u32[]{:S(2)}) %collective-permute-start) | collective-permute-done | bytes 2048032 | tf_op jit(solution)/shard_map/cond/branch_1_fun/ppermute | solution.py:39
  21.5 0.7 conditional
  21.5 0.7 reshape.32
  22.2 4.6 %collective-permute-done.1 = bf16[4,500,512]{2,0,1:T(4,128)(2,1)S(1)} collective-permute-done((bf16[4,500,512]{2,0,1:T(4,128)(2,1)}, bf16[4,500,512]{2,0,1:T(4,128)(2,1)S(1)}, u32[]{:S(2)}, u32[]{:S(2)}) %collective-permute-start.1) | collective-permute-done | bytes 2048032 | tf_op jit(solution)/shard_map/ppermute | solution.py:39
  26.9 39.3 %conditional.5 = (f32[192,128]{1,0:T(8,128)S(1)}, f32[768,128]{1,0:T(8,128)S(1)}) conditional(s32[]{:T(128)} %clamp.4, (bf16[4,500,512]{2,0,1:T(4,128)(2,1)}, bf16[4,500,512]{2,0,1:T(4,128)(2,1)}, bf16[4,500,512]{2,0,1:T(4,128)(2,1)S(1)}, s32[2]{0:T(128)S(1)}, f32[32,12,128]{2,1,0:T(8,128)}) %tuple.46, ...), branch_computations={%region_5.8_spmd, %region_8.10_spmd, %region_10.11_spmd} | conditional | flops 1605414912 | bytes 18010724 | solution.py:261
  26.9 6.9 %branch_1_fun.1 = f32[8,776,128]{2,1,0:T(8,128)S(1)} custom-call(s32[2]{0:T(128)S(1)} %get-tuple-element.67.flags, bf16[500,4,512]{2,1,0:T(4,128)(2,1)} %bitcast.45, bf16[500,4,512]{2,1,0:T(4,128)(2,1)} %bitcast.9.beside, bf16[500,4,512]{2,1,0:T(4,128)(2,1)S(1)} %bitcast.48), custom_call_target="tpu_custom_call" | custom-call | flops 1600000000 | bytes 8000000 | tf_op jit(solution)/shard_map/cond/branch_1_fun/pallas_call | solution.py:197
  33.8 0.2 convert_element_type.51
  34.0 30.7 %all_to_all.22 = f16[8,776,128]{2,1,0:T(8,128)(2,1)S(1)} all-to-all(f16[8,776,128]{2,1,0:T(8,128)(2,1)S(1)} %convert_element_type.51), channel_id=1, replica_groups=mesh['zl'=4,'y'=8,'zh'=2,'x'=4,'c'=2] {'y'}, dimensions={0} | all-to-all | bytes 3178496 | tf_op jit(solution)/shard_map/cond/branch_1_fun/all_to_all | solution.py:234
  64.7 0.2 fusion.30
  64.9 0.8 fusion.26
  66.2 0.0 collective-permute-done.2
  66.2 12.6 %conditional.6 = (f32[192,128]{1,0:T(8,128)S(1)}) conditional(s32[]{:T(128)} %clamp.4, f32[192,128]{1,0:T(8,128)S(1)} %get-tuple-element.91, f32[768,128]{1,0:T(8,128)S(1)} %get-tuple-element.92, (bf16[4,500,512]{2,0,1:T(4,128)(2,1)}, bf16[4,500,512]{2,0,1:T(4,128)(2,1)}, bf16[4,500,512]{2,0,1:T(4,128)(2,1)}, s32[2]{0:T(128)S(1)}, ...), branch_computations={%region_11.12_spmd, %region_12.14_spmd, %region_14.17_spmd} | conditional | flops 1603137792 | bytes 14259340 | solution.py:270
  66.2 12.5 %all_to_all.23 = f32[4,192,128]{2,1,0:T(8,128)S(1)} all-to-all(f32[4,192,128]{2,1,0:T(8,128)S(1)} %bitcast.49), channel_id=1, replica_groups=mesh['zl'=4,'y'=8,'zh'=2,'x'=4,'c'=2] {'zl'}, dimensions={0} | all-to-all | bytes 786432 | tf_op jit(solution)/shard_map/cond/branch_1_fun/all_to_all | solution.py:257
  78.8 7.1 %collective-permute-start.4 = (f32[96,128]{1,0:T(8,128)S(1)}, f32[96,128]{1,0:T(8,128)S(1)}, u32[]{:S(2)}, u32[]{:S(2)}) collective-permute-start(f32[96,128]{1,0:T(8,128)S(1)} %slice.101), channel_id=1, source_target_pairs={{1,15},{3,1},{5,3},{7,5},{9,7},{11,9},{13,11},{15,13},{17,31},{19,... | collective-permute-start | bytes 147464 | tf_op jit(solution)/shard_map/ppermute | solution.py:39
  86.0 10.7 %collective-permute-start.3 = (f32[32,128]{1,0:T(8,128)S(1)}, f32[32,128]{1,0:T(8,128)S(1)}, u32[]{:S(2)}, u32[]{:S(2)}) collective-permute-start(f32[32,128]{1,0:T(8,128)S(1)} %slice_select_fusion.2), channel_id=1, source_target_pairs={{0,1},{1,0},{2,3},{3,2},{4,5},{5,4},{6,7},{7,6},{8,9},{9,8},{10,11... | collective-permute-start | bytes 49160 | tf_op jit(solution)/shard_map/ppermute | solution.py:39
  96.7 0.8 collective-permute-done.3
  97.5 3.7 %collective-permute-done.4 = f32[96,128]{1,0:T(8,128)S(1)} collective-permute-done((f32[96,128]{1,0:T(8,128)S(1)}, f32[96,128]{1,0:T(8,128)S(1)}, u32[]{:S(2)}, u32[]{:S(2)}) %collective-permute-start.4) | collective-permute-done | bytes 49184 | tf_op jit(solution)/shard_map/ppermute | solution.py:39
  101.2 0.6 pad_maximum_fusion.2
  (7 shorter events, 0.1 us)
Async XLA Ops:
  0.0 26.9 %collective-permute-start.1 = (bf16[4,500,512]{2,0,1:T(4,128)(2,1)}, bf16[4,500,512]{2,0,1:T(4,128)(2,1)S(1)}, u32[]{:S(2)}, u32[]{:S(2)}) collective-permute-start(bf16[4,500,512]{2,0,1:T(4,128)(2,1)} %param.11), channel_id=1, source_target_pairs={{1,3},{2,0},{3,5},{4,2},{5,7},{6,4},{9,11},{10,8},{11,13},{12,10},... | collective-permute-start | bytes 6144008 | tf_op jit(solution)/shard_map/ppermute | solution.py:39
  1.3 64.9 %collective-permute-start.2 = (bf16[4,500,512]{2,0,1:T(4,128)(2,1)}, bf16[4,500,512]{2,0,1:T(4,128)(2,1)}, u32[]{:S(2)}, u32[]{:S(2)}) collective-permute-start(bf16[4,500,512]{2,0,1:T(4,128)(2,1)} %param.11), channel_id=1, source_target_pairs={{0,14},{7,9},{8,6},{15,1},{16,30},{23,25},{24,22},{31,17},{32,46},... | collective-permute-start | bytes 6144008 | tf_op jit(solution)/shard_map/ppermute | solution.py:39
  15.2 6.3 %collective-permute-start = (bf16[4,500,512]{2,0,1:T(4,128)(2,1)}, bf16[4,500,512]{2,0,1:T(4,128)(2,1)}, u32[]{:S(2)}, u32[]{:S(2)}) collective-permute-start(bf16[4,500,512]{2,0,1:T(4,128)(2,1)} %get-tuple-element.60), channel_id=1, source_target_pairs={{0,1},{1,0},{2,3},{3,2},{4,5},{5,4},{6,7},{7,6},{8,9},{9,8},{10,11... | collective-permute-start | bytes 6144008 | tf_op jit(solution)/shard_map/cond/branch_1_fun/ppermute | solution.py:39
  78.8 22.4 %collective-permute-start.4 = (f32[96,128]{1,0:T(8,128)S(1)}, f32[96,128]{1,0:T(8,128)S(1)}, u32[]{:S(2)}, u32[]{:S(2)}) collective-permute-start(f32[96,128]{1,0:T(8,128)S(1)} %slice.101), channel_id=1, source_target_pairs={{1,15},{3,1},{5,3},{7,5},{9,7},{11,9},{13,11},{15,13},{17,31},{19,... | collective-permute-start | bytes 147464 | tf_op jit(solution)/shard_map/ppermute | solution.py:39
  86.0 11.5 %collective-permute-start.3 = (f32[32,128]{1,0:T(8,128)S(1)}, f32[32,128]{1,0:T(8,128)S(1)}, u32[]{:S(2)}, u32[]{:S(2)}) collective-permute-start(f32[32,128]{1,0:T(8,128)S(1)} %slice_select_fusion.2), channel_id=1, source_target_pairs={{0,1},{1,0},{2,3},{3,2},{4,5},{5,4},{6,7},{7,6},{8,9},{9,8},{10,11... | collective-permute-start | bytes 49160 | tf_op jit(solution)/shard_map/ppermute | solution.py:39
